TPU v7x, 1024 devices: a whole 4x4x32 slice. The times are simulated.
1024 devices in a mesh: dp: 64 (over x, z_lo), fsdp: 16 (over z_hi, y, core).
Axes of the slice: x: 4, y: 4, z: 32 (z_hi: 2, z_lo: 16; z = z_hi * 16 + z_lo), core: 2. Of those that a mesh axis runs over, the one named last changes fastest.
Arguments:
- embeddings: bfloat16 [1024, 256, 256], P(('dp', 'fsdp')), may hold values from -6 to 6
- cotangent: bfloat16 [1024, 256, 256], P(('dp', 'fsdp')), may hold values from -24 to 24
- owners: int32 [1024, 256], P(('dp', 'fsdp')), may hold values from 0 to 63, as said below
- projection: bfloat16 [256, 128], P('fsdp'), may hold values from -0.375 to 0.375
- up_weight: bfloat16 [128, 4096], P('fsdp'), may hold values from -0.5 to 0.5
- down_weight: bfloat16 [4096, 256], P('fsdp'), may hold values from -0.09375 to 0.09375
Outputs:
- owned_grads: bfloat16 [262144, 256], P(('dp', 'fsdp'))
- grad_projection: float32 [256, 128], P('fsdp')
- grad_up: float32 [128, 4096], P('fsdp')
- grad_down: float32 [4096, 256], P('fsdp')
Inputs may be any that keep to these rules, and one draw needn't show every extreme that they name: `owners`: among the rows (samples by features) of one device, every owner appears exactly 1 * 256 / 64 times.
All inputs are finite; a program needn't handle non-finite values.
Results may differ from a plain program's by a relative error of at most 0.018.
Values may be sent and summed in bfloat16 or wider, within the bound.
A program may use at most 32 MiB of HBM per device.

v0:
```python
import jax
import jax.numpy as jnp
from jax import lax
from jax.sharding import PartitionSpec as P


def local_backward(emb, cot, proj, w_up, w_down):
    samples, feats, width = emb.shape
    rank = proj.shape[1]
    compressed = jnp.einsum("sfd,fk->sdk", emb, proj, preferred_element_type=jnp.float32).astype(
        jnp.bfloat16
    )
    fm_vals = jnp.einsum("sfd,sdk->sfk", emb, compressed, preferred_element_type=jnp.float32)
    centre = fm_vals - jnp.mean(fm_vals, axis=-1, keepdims=True)
    inv = lax.rsqrt(jnp.mean(centre * centre, axis=-1, keepdims=True) + 1e-05)
    normed = centre * inv
    normed_low = normed.astype(jnp.bfloat16).reshape(samples * feats, rank)
    cot_rows = cot.reshape(samples * feats, width)
    hidden = jnp.dot(normed_low, w_up, preferred_element_type=jnp.float32)
    sig = jax.nn.sigmoid(hidden)
    activated = (hidden * sig).astype(jnp.bfloat16)
    grad_act = jnp.einsum("rd,hd->rh", cot_rows, w_down, preferred_element_type=jnp.float32)
    grad_hidden = (grad_act * sig * (1.0 + hidden * (1.0 - sig))).astype(jnp.bfloat16)
    grad_normed = jnp.einsum(
        "rh,kh->rk", grad_hidden, w_up, preferred_element_type=jnp.float32
    ).reshape(samples, feats, rank)
    grad_fm = inv * (
        grad_normed
        - jnp.mean(grad_normed, axis=-1, keepdims=True)
        - normed * jnp.mean(grad_normed * normed, axis=-1, keepdims=True)
    )
    grad_fm = grad_fm.astype(jnp.bfloat16)
    grad_comp = jnp.einsum("sfd,sfk->sdk", emb, grad_fm, preferred_element_type=jnp.float32).astype(
        jnp.bfloat16
    )
    grad_embed = (
        jnp.einsum("sfk,sdk->sfd", grad_fm, compressed, preferred_element_type=jnp.float32)
        + jnp.einsum("fk,sdk->sfd", proj, grad_comp, preferred_element_type=jnp.float32)
    ).astype(jnp.bfloat16)
    part_up = jnp.einsum("rk,rh->kh", normed_low, grad_hidden, preferred_element_type=jnp.float32)
    part_down = jnp.einsum("rh,rd->hd", activated, cot_rows, preferred_element_type=jnp.float32)
    part_proj = jnp.einsum("sfd,sdk->fk", emb, grad_comp, preferred_element_type=jnp.float32)
    return (grad_embed, part_proj, part_up, part_down)


def per_device(embeddings, cotangent, owners, projection, up_weight, down_weight):
    samples, feats, width = embeddings.shape
    proj_all, up_all, down_all = (
        lax.all_gather(projection, "fsdp", axis=0, tiled=True),
        lax.all_gather(up_weight, "fsdp", axis=0, tiled=True),
        lax.all_gather(down_weight, "fsdp", axis=0, tiled=True),
    )
    grad_embed, part_proj, part_up, part_down = local_backward(
        embeddings, cotangent, proj_all, up_all, down_all
    )
    share_proj, share_up, share_down = (
        lax.psum_scatter(
            part_proj.astype(jnp.bfloat16), "fsdp", scatter_dimension=0, tiled=True
        ).astype(jnp.float32),
        lax.psum_scatter(
            part_up.astype(jnp.bfloat16), "fsdp", scatter_dimension=0, tiled=True
        ).astype(jnp.float32),
        lax.psum_scatter(
            part_down.astype(jnp.bfloat16), "fsdp", scatter_dimension=0, tiled=True
        ).astype(jnp.float32),
    )
    total_proj, total_up, total_down = lax.psum((share_proj, share_up, share_down), "dp")
    scale = 1.0 / (samples * lax.axis_size("dp") * lax.axis_size("fsdp"))
    groups = lax.axis_size("dp")
    rows = samples * feats
    per_owner = rows // groups
    owner_flat = owners.reshape(rows)
    onehot = (owner_flat[:, None] == jnp.arange(groups, dtype=jnp.int32)[None, :]).astype(jnp.int32)
    running = jnp.cumsum(onehot, axis=0) - 1
    within = jnp.sum(onehot * running, axis=1)
    target = owner_flat * per_owner + within
    outgoing = (
        jnp.zeros((rows, width), jnp.bfloat16).at[target].set(grad_embed.reshape(rows, width))
    )
    owned = lax.all_to_all(outgoing, "dp", split_axis=0, concat_axis=0, tiled=True)
    return (owned, total_proj * scale, total_up * scale, total_down * scale)


def solution(mesh):
    return jax.shard_map(
        per_device,
        mesh=mesh,
        in_specs=(
            P(("dp", "fsdp"), None, None),
            P(("dp", "fsdp"), None, None),
            P(("dp", "fsdp"), None),
            P("fsdp", None),
            P("fsdp", None),
            P("fsdp", None),
        ),
        out_specs=(P(("dp", "fsdp"), None), P("fsdp", None), P("fsdp", None), P("fsdp", None)),
        check_vma=False,
    )
```

profile of v0, /device:TPU:24, one launch (start us, length us, event | category | flops | bytes accessed | tf_op | source)
XLA Modules:
  0.0 1498.6 jit_solution(7939590328486438690)
XLA Ops:
  7.2 0.0 copy-start
  7.2 0.0 all-gather.5.cloned.1.call-start
  7.2 0.7 all-gather.5.cloned.1.call-update
  7.9 0.0 all-gather.3.cloned.1.call-start
  8.0 0.7 all-gather.3.cloned.1.call-update
  8.7 0.0 reduce-scatter.10.cloned.1.call-start
  8.7 59.2 %all_gather.9 = bf16[256,128]{1,0:T(8,128)(2,1)S(1)} all-gather(bf16[16,128]{1,0:T(8,128)(2,1)} %param.9), channel_id=1, replica_groups=mesh['dp'=64,'fsdp'=16] {'fsdp'}, dimensions={0}, use_global_device_ids=true | all-gather | bytes 69632 | tf_op jit(solution)/shard_map/all_gather | solution.py:49
  68.0 0.0 copy-start.3
  68.0 0.6 copy-done.3
  68.6 1.1 convolution_convert_fusion.4
  69.7 0.0 copy-start.5
  69.7 0.6 copy-done.5
  70.3 1.1 fusion.25
  71.5 70.6 %all-gather.5.cloned.1.call-done = bf16[128,4096]{1,0:T(8,128)(2,1)} async-done(((bf16[8,4096]{1,0:T(8,128)(2,1)}), bf16[128,4096]{1,0:T(8,128)(2,1)}) %all-gather.5.cloned.1.call-update) | async-done | bytes 1048592 | tf_op jit(solution)/shard_map/all_gather | solution.py:50
  142.2 3.9 fusion.22
  146.0 0.0 copy-start.1
  146.0 0.0 copy-start.2
  146.0 132.2 %all-gather.3.cloned.1.call-done = bf16[4096,256]{1,0:T(8,128)(2,1)} async-done(((bf16[256,256]{1,0:T(8,128)(2,1)}), bf16[4096,256]{1,0:T(8,128)(2,1)}) %all-gather.3.cloned.1.call-update) | async-done | bytes 2097168 | tf_op jit(solution)/shard_map/all_gather | solution.py:51
  278.2 0.0 copy-done
  278.2 4.7 fusion.1
  282.9 0.0 copy-done.1
  282.9 0.9 fusion.24
  283.8 0.0 copy-done.2
  283.8 0.2 convolution_convert_fusion.3
  284.0 0.2 fusion.5
  284.2 0.7 copy.19
  284.9 0.0 reduce-scatter.10.cloned.1.call-update
  284.9 0.0 copy-start.7
  284.9 0.0 reduce-scatter.8.cloned.1.call-start
  285.0 5.1 convolution_convert_fusion
  290.1 0.0 copy-start.4
  290.1 0.0 copy-start.6
  290.1 0.0 reduce-scatter.8.cloned.1.call-update
  290.1 0.0 reduce-scatter.6.cloned.1.call-start
  290.2 0.0 copy-done.7
  290.2 0.6 reduce-window.6
  290.8 0.2 slice_reduce_fusion
  291.0 1.4 convolution_convert_fusion.1
  292.5 0.0 reduce-scatter.6.cloned.1.call-update
  292.5 0.1 fusion.18
  292.6 0.0 copy-done.4
  292.6 0.2 convolution_bitcast_fusion
  292.8 0.0 copy-done.6
  292.8 0.2 fusion.4
  293.0 1.5 scatter_custom_fusion
  294.5 0.7 all_to_all.8
  295.2 5.7 all-to-all-start
  301.0 99.4 %reduce-scatter.10.cloned.1.call-done = bf16[16,128]{1,0:T(8,128)(2,1)} async-done(((bf16[256,128]{1,0:T(8,128)(2,1)}), bf16[16,128]{1,0:T(8,128)(2,1)}) %reduce-scatter.10.cloned.1.call-update) | async-done | bytes 4112
  400.3 0.8 copy.20
  401.1 0.0 all-to-all-done
  401.1 0.7 all_to_all.10
  401.8 177.2 %reduce-scatter.8.cloned.1.call-done = bf16[256,256]{1,0:T(8,128)(2,1)} async-done(((bf16[4096,256]{1,0:T(8,128)(2,1)}), bf16[256,256]{1,0:T(8,128)(2,1)}) %reduce-scatter.8.cloned.1.call-update) | async-done | bytes 131088 | tf_op jit(solution)/shard_map/reduce_scatter | solution.py:63
  579.0 148.5 %reduce-scatter.6.cloned.1.call-done = bf16[8,4096]{1,0:T(8,128)(2,1)} async-done(((bf16[128,4096]{1,0:T(8,128)(2,1)}), bf16[8,4096]{1,0:T(8,128)(2,1)}) %reduce-scatter.6.cloned.1.call-update) | async-done | bytes 65552 | tf_op jit(solution)/shard_map/reduce_scatter | solution.py:60
  727.6 762.4 %all-reduce.2 = (f32[16,128]{0,1:T(8,128)S(1)}, f32[8,4096]{1,0:T(8,128)S(1)}, f32[256,256]{1,0:T(8,128)S(1)}) all-reduce(bf16[16,128]{0,1:T(8,128)(2,1)S(1)} %copy.20, bf16[8,4096]{1,0:T(8,128)(2,1)} %reduce-scatter.6.cloned.1.call-done, bf16[256,256]{1,0:T(8,128)(2,1)} %reduce-scatter.8.cloned.1.call-done), channel_id=1, replica_groups=mesh['dp'=64,'fsdp'=16] {'dp'}, use_global_device_ids=true, to_apply=%region_9.0 | all-reduce | flops 100352 | bytes 602112 | tf_op jit(solution)/shard_map/psum | solution.py:67
  1490.0 0.7 broadcast_multiply_fusion
  1490.7 0.7 broadcast_multiply_fusion.1
  1491.4 0.7 copy.17
  (10 shorter events, 0.2 us)
Async XLA Ops:
  7.2 271.0 %copy-start = (bf16[1,256,256]{2,1,0:T(8,128)(2,1)S(1)}, bf16[1,256,256]{2,1,0:T(8,128)(2,1)}, u32[]{:S(2)}) copy-start(bf16[1,256,256]{2,1,0:T(8,128)(2,1)} %param.7) | copy-start | bytes 393220
  7.2 135.0 %all-gather.5.cloned.1.call-start = ((), (), s32[]{:S(2)}) async-start(), calls=%async_computation.5 | async-start | bytes 1114112 | tf_op jit(solution)/shard_map/all_gather | solution.py:50
  7.9 270.3 %all-gather.3.cloned.1.call-start = ((), (), s32[]{:S(2)}) async-start(), calls=%async_computation.4 | async-start | bytes 2228224 | tf_op jit(solution)/shard_map/all_gather | solution.py:51
  8.7 391.7 %reduce-scatter.10.cloned.1.call-start = ((), (), s32[]{:S(2)}) async-start(), calls=%async_computation.8 | async-start | bytes 69632
  68.0 0.6 copy-start.3
  69.7 0.6 copy-start.5
  146.0 136.8 %copy-start.1 = (bf16[128,4096]{1,0:T(8,128)(2,1)S(1)}, bf16[128,4096]{1,0:T(8,128)(2,1)}, u32[]{:S(2)}) copy-start(bf16[128,4096]{1,0:T(8,128)(2,1)} %all-gather.5.cloned.1.call-done) | copy-start | bytes 3145732
  146.0 137.8 %copy-start.2 = (bf16[1,256,256]{2,1,0:T(8,128)(2,1)S(1)}, bf16[1,256,256]{2,1,0:T(8,128)(2,1)}, u32[]{:S(2)}) copy-start(bf16[1,256,256]{2,1,0:T(8,128)(2,1)} %param.6) | copy-start | bytes 393220
  284.9 5.2 copy-start.7
  284.9 294.1 %reduce-scatter.8.cloned.1.call-start = ((), (), s32[]{:S(2)}) async-start(), calls=%async_computation.7 | async-start | bytes 2228224 | tf_op jit(solution)/shard_map/reduce_scatter | solution.py:63
  290.1 2.5 copy-start.4
  290.1 2.7 copy-start.6
  290.1 437.4 %reduce-scatter.6.cloned.1.call-start = ((), (), s32[]{:S(2)}) async-start(), calls=%async_computation.6 | async-start | bytes 1114112 | tf_op jit(solution)/shard_map/reduce_scatter | solution.py:60
  295.2 105.9 %all-to-all-start = ((bf16[64,4,256]{2,1,0:T(4,128)(2,1)}), bf16[64,4,256]{2,1,0:T(4,128)(2,1)S(1)}, u32[]{:S(2)}, u32[]{:S(2)}) async-start(bf16[64,4,256]{2,1,0:T(4,128)(2,1)} %all_to_all.8), calls=%async_computation | async-start | bytes 262144 | tf_op jit(solution)/shard_map/all_to_all | solution.py:80
Sparse Core Ops, SparseCore 0:
  12.5 129.6 all-gather.4
  146.6 131.5 all-gather.2
  285.1 115.2 reduce-scatter.9
  406.2 172.8 reduce-scatter.7
  584.7 142.7 reduce-scatter.5
where the time goes:
time: 1500 us
  blocking collectives  822 us (55%)
  waiting for transfers between devices  629 us (42%)
  matrix products  18.9 us (1%)
    psum x1, blocking collectives, per_device(): lax.psum((share_proj, share_up, share_down), 'dp')  762 us
    reduce_scatter x1, waiting for transfers between devices, per_device(): lax.psum_scatter(part_down.astype(jnp.bfloat16), 'fsdp', scatter_dimensio...  177 us
    reduce_scatter x1, waiting for transfers between devices, per_device(): lax.psum_scatter(part_up.astype(jnp.bfloat16), 'fsdp', scatter_dimension=...  149 us
    all_gather x1, waiting for transfers between devices, per_device(): lax.all_gather(down_weight, 'fsdp', axis=0, tiled=True)  132 us
    unnamed x6, waiting for transfers between devices  101 us
    all_gather x1, waiting for transfers between devices, per_device(): lax.all_gather(up_weight, 'fsdp', axis=0, tiled=True)  70.6 us
    all_gather x1, blocking collectives, per_device(): lax.all_gather(projection, 'fsdp', axis=0, tiled=True)  59.2 us
  transfers between devices with their start and end apart: 6, of which 5 were waited for; matrix products, arithmetic and copies ran while one was open for 1% of the time, Pallas kernels for 0%

commit v1 on v0

v1 whole, which is shorter than its diff:
```python
import functools

import jax
import jax.numpy as jnp
from jax import lax
from jax.experimental import pallas as pl
from jax.experimental.pallas import tpu as pltpu
from jax.sharding import PartitionSpec as P

BF = jnp.bfloat16
F32 = jnp.float32
SPLITS = {64: (4, 16, 4), 4: (2, 2, 2), 8: (2, 4, 2)}
NZH, NY, NC = 2, 4, 2
NF = NZH * NY * NC
MAIN, ROWS = 768, 784


def mm(a, b, ca=1, cb=0):
    return lax.dot_general(a, b, (((ca,), (cb,)), ((), ())), preferred_element_type=F32)


def kernel(
    split, x_ref, cot_ref, own_ref, proj_ref, up_ref, dn_ref,
    owned_ref, gproj_ref, gup_ref, gdn_ref,
    wg, gg, rc, sa, ry, sb, rx, sc, rq, se, rb, ox, nl, gn, av1, av2, av3, av4,
    ag_s, ag_r, rs_s, rs_r, aa_s, aa_r,
):
    nx, nzl, nq = split
    nb = nzl // nq
    feats = x_ref.shape[1]
    xp = rx.shape[2]
    bp = rb.shape[1]
    qp = nb * bp
    zrows = feats // nzl
    per = zrows // nx
    dp, fs = lax.axis_index("dp"), lax.axis_index("fsdp")
    x, zl = dp // nzl, dp % nzl
    zh, y, c = fs // (NY * NC), (fs // NC) % NY, fs % NC
    q, b = zl % nq, zl // nq

    def dev(x=x, zl=zl, zh=zh, y=y, c=c):
        return {"dp": x * nzl + zl, "fsdp": (zh * NY + y) * NC + c}

    pending = []

    def send(src, dst, sems, to):
        ssem, rsem, i = sems
        copy = pltpu.make_async_remote_copy(
            src_ref=src, dst_ref=dst, send_sem=ssem.at[i], recv_sem=rsem.at[i],
            device_id=to, device_id_type=pl.DeviceIdType.MESH,
        )
        copy.start()
        pending.append(copy)
        return copy

    barrier = pltpu.get_barrier_semaphore()
    peers = [dev(c=1 - c)]
    peers += [dev(y=(y + k) % NY) for k in range(1, NY)]
    peers += [dev(x=(x + k) % nx) for k in range(1, nx)]
    peers += [dev(zl=(zl + k) % nzl) for k in range(1, nzl)]
    peers += [dev(zh=1 - zh, zl=((b + k) % nb) * nq + q) for k in range(nb)]
    peers += [dev(zh=1 - zh, zl=nzl - 1 - zl)]
    for p in peers:
        pl.semaphore_signal(barrier, inc=1, device_id=p, device_id_type=pl.DeviceIdType.MESH)

    wg[fs, 0:256] = dn_ref[:, 0:128]
    wg[fs, 256:512] = dn_ref[:, 128:256]
    for u in range(NF):
        lo = up_ref[:, 256 * u : 256 * u + 128].astype(F32)
        hi = up_ref[:, 256 * u + 128 : 256 * u + 256].astype(F32)
        wg[fs, 512 + 16 * u : 528 + 16 * u] = jnp.concatenate([lo, hi], axis=0).astype(BF)
    wg[fs, MAIN:ROWS] = proj_ref[...]
    pl.semaphore_wait(barrier, len(peers))

    part = MAIN // (nx * nq)
    fp = fs + (1 - 2 * zh) * NY * NC
    mq = nq - 1 - q
    piece = pl.ds(pl.multiple_of((x * nq + mq) * part, 16), part)
    n_ag = 0
    across = [
        send(wg.at[fs, piece], wg.at[fs, piece], (ag_s, ag_r, 0), dev(zh=1 - zh, zl=nzl - 1 - zl)),
        send(wg.at[fs, MAIN:ROWS], wg.at[fs, MAIN:ROWS], (ag_s, ag_r, 1), dev(zh=1 - zh, zl=nzl - 1 - zl)),
    ]
    n_ag = 2
    ycopies = []
    for k in (1, 3, 2):
        ycopies.append((k, fs, send(wg.at[fs], wg.at[fs], (ag_s, ag_r, n_ag), dev(y=(y + k) % NY))))
        n_ag += 1
    ccopies = [send(wg.at[fs], wg.at[fs], (ag_s, ag_r, n_ag), dev(c=1 - c))]
    n_ag += 1
    across[0].wait_recv()
    piece = pl.ds(pl.multiple_of((x * nq + q) * part, 16), part)
    step = []
    for k in range(1, nq):
        step.append(send(wg.at[fp, piece], wg.at[fp, piece], (ag_s, ag_r, n_ag), dev(zl=b * nq + (q + k) % nq)))
        n_ag += 1
    for s in step:
        s.wait_recv()
    piece = pl.ds(pl.multiple_of(x * nq * part, 16), nq * part)
    step = []
    for k in range(1, nx):
        step.append(send(wg.at[fp, piece], wg.at[fp, piece], (ag_s, ag_r, n_ag), dev(x=(x + k) % nx)))
        n_ag += 1
    for s in step:
        s.wait_recv()
    across[1].wait_recv()
    for k in (1, 3, 2):
        ycopies.append((k, fp, send(wg.at[fp], wg.at[fp], (ag_s, ag_r, n_ag), dev(y=(y + k) % NY))))
        n_ag += 1
    ccopies.append(send(wg.at[fp], wg.at[fp], (ag_s, ag_r, n_ag), dev(c=1 - c)))
    n_ag += 1
    for k, base, copy in ycopies:
        copy.wait_recv()
        got = base + (((y - k + NY) % NY) - y) * NC
        ccopies.append(send(wg.at[got], wg.at[got], (ag_s, ag_r, n_ag), dev(c=1 - c)))
        n_ag += 1
    for s in ccopies:
        s.wait_recv()

    emb, cot = x_ref[0], cot_ref[0]
    proj = wg[:, MAIN:ROWS, :].reshape(feats, 128)
    compressed = mm(emb, proj, 0, 0).astype(BF)
    fm = mm(emb, compressed)
    centre = fm - jnp.mean(fm, axis=-1, keepdims=True)
    inv = lax.rsqrt(jnp.mean(centre * centre, axis=-1, keepdims=True) + 1e-05)
    normed = centre * inv
    nl[...] = normed.astype(BF)
    gn[...] = jnp.zeros_like(gn)

    @pl.loop(0, NF)
    def _(u):
        urows = pl.ds(pl.multiple_of(512 + 16 * u, 16), 16)
        pieces = wg[:, urows, :].astype(F32)
        up = jnp.concatenate(
            [pieces[:, 0:8].reshape(128, 128), pieces[:, 8:16].reshape(128, 128)], axis=1
        ).astype(BF)
        down = jnp.concatenate([wg[u, 0:256], wg[u, 256:512]], axis=1)
        low, cots = nl[...], cot_ref[0]
        hidden = mm(low, up)
        sig = 0.5 * jnp.tanh(0.5 * hidden) + 0.5
        act = (hidden * sig).astype(BF)
        gh = (mm(cots, down, 1, 1) * sig * (1.0 + hidden * (1.0 - sig))).astype(BF)
        gn[...] += mm(gh, up, 1, 1)
        gup = mm(low, gh, 0, 0)
        gup = jnp.concatenate(
            [gup[:, 0:128].reshape(NF, 8, 128), gup[:, 128:256].reshape(NF, 8, 128)], axis=1
        ).astype(BF)
        gg[:, :, :, urows, :] = gup.reshape(NZH, NY, NC, 16, 128)
        gdn = mm(act, cots, 0, 0).astype(BF)
        at = (u // (NY * NC), (u // NC) % NY, u % NC)
        gg[at[0], at[1], at[2], 0:256] = gdn[:, 0:128]
        gg[at[0], at[1], at[2], 256:512] = gdn[:, 128:256]

    rs = 0
    main = pl.ds(0, MAIN)
    tail = pl.ds(MAIN, ROWS - MAIN)
    r0 = [send(gg.at[:, :, 1 - c, main], rc.at[:, :, main], (rs_s, rs_r, rs), dev(c=1 - c))]
    rs += 1

    gnorm = gn[...]
    gfm = inv * (
        gnorm
        - jnp.mean(gnorm, axis=-1, keepdims=True)
        - normed * jnp.mean(gnorm * normed, axis=-1, keepdims=True)
    )
    gfm = gfm.astype(BF)
    gcomp = mm(emb, gfm, 0, 0).astype(BF)
    gproj = mm(emb, gcomp).astype(BF)
    gg[:, :, :, MAIN:ROWS, :] = gproj.reshape(NZH, NY, NC, 16, 128)
    r0.append(send(gg.at[:, :, 1 - c, tail], rc.at[:, :, tail], (rs_s, rs_r, rs), dev(c=1 - c)))
    rs += 1
    gemb = (mm(gfm, compressed, 1, 1) + mm(proj, gcomp, 1, 1)).astype(BF)

    row = lax.broadcasted_iota(jnp.int32, (feats, feats), 0)
    col = lax.broadcasted_iota(jnp.int32, (feats, feats), 1)
    across_f = jnp.broadcast_to(own_ref[...].astype(F32), (feats, feats))
    down_f = jnp.sum(jnp.where(row == col, across_f, 0.0), axis=1, keepdims=True)
    within = jnp.sum(
        jnp.where((across_f == down_f) & (row < col), 1.0, 0.0), axis=0, keepdims=True
    )
    owner = across_f[0:1]
    owner_x = jnp.floor(owner * (1.0 / nzl))
    place = (owner - owner_x * nzl) * zrows + owner_x * per + within
    perm = jnp.where(row.astype(F32) == place, 1.0, 0.0).astype(BF)
    av1[...] = mm(perm, gemb).astype(BF)
    a1 = []
    mine = pl.ds(pl.multiple_of(zl * zrows, 16), zrows)
    aa = 0
    for k in range(1, nzl):
        to = (zl + k) % nzl
        theirs = pl.ds(pl.multiple_of(to * zrows, 16), zrows)
        a1.append(send(av1.at[theirs], av2.at[mine], (aa_s, aa_r, aa), dev(zl=to)))
        aa += 1
    av2[mine] = av1[mine]

    for s in r0:
        s.wait_recv()
    blk = 112
    r1 = []
    for k in (1, 3, 2, 0):
        to = (y + k) % NY

        @pl.loop(0, ROWS // blk)
        def _(i, to=to):
            r = pl.ds(pl.multiple_of(i * blk, 16), blk)
            sa[to, :, r] = (gg[:, to, c, r].astype(F32) + rc[:, to, r].astype(F32)).astype(BF)

        if k:
            r1.append(send(sa.at[to], ry.at[k - 1], (rs_s, rs_r, rs), dev(y=to)))
            rs += 1

    for s in a1:
        s.wait_recv()
    r_z, r_x, r_k = col // zrows, (col % zrows) // per, col % per
    perm = jnp.where(row == r_x * (nzl * per) + r_z * per + r_k, 1.0, 0.0).astype(BF)
    av3[...] = mm(perm, av2[...]).astype(BF)
    a2 = []
    xrows = nzl * per
    mine = pl.ds(pl.multiple_of(x * xrows, 16), xrows)
    for k in range(1, nx):
        to = (x + k) % nx
        theirs = pl.ds(pl.multiple_of(to * xrows, 16), xrows)
        a2.append(send(av3.at[theirs], av4.at[mine], (aa_s, aa_r, aa), dev(x=to)))
        aa += 1
    av4[mine] = av3[mine]

    for s in r1:
        s.wait_recv()
    if sb.shape[1] > ROWS:
        sb[:, ROWS:] = jnp.zeros((NZH, sb.shape[1] - ROWS, 128), BF)

    @pl.loop(0, ROWS // blk)
    def _(i):
        r = pl.ds(pl.multiple_of(i * blk, 16), blk)
        t = sa[y, :, r].astype(F32)
        for k in range(NY - 1):
            t += ry[k, :, r].astype(F32)
        sb[:, r] = t.astype(BF)

    r2 = []
    for k in range(1, nx):
        to = (x + k) % nx
        theirs = pl.ds(pl.multiple_of(to * xp, 16), xp)
        r2.append(send(sb.at[:, theirs], rx.at[k - 1], (rs_s, rs_r, rs), dev(x=to)))
        rs += 1
    for s in r2:
        s.wait_recv()
    t = sb[:, pl.ds(pl.multiple_of(x * xp, 16), xp)].astype(F32)
    for k in range(nx - 1):
        t += rx[k].astype(F32)
    sc[:, 0:xp] = t.astype(BF)
    if sc.shape[1] > xp:
        sc[:, xp:] = jnp.zeros((NZH, sc.shape[1] - xp, 128), BF)

    r3 = []
    for k in range(1, nq):
        to = (q + k) % nq
        theirs = pl.ds(pl.multiple_of(to * qp, 16), qp)
        r3.append(send(sc.at[:, theirs], rq.at[k - 1], (rs_s, rs_r, rs), dev(zl=b * nq + to)))
        rs += 1
    for s in r3:
        s.wait_recv()
    t = sc[:, pl.ds(pl.multiple_of(q * qp, 16), qp)].astype(F32)
    for k in range(nq - 1):
        t += rq[k].astype(F32)
    se[...] = t.astype(BF)

    r4 = []
    for k in range(1, NZH * nb):
        h2, b2 = (zh + k // nb) % NZH, (b + k % nb) % nb
        theirs = pl.ds(pl.multiple_of(b2 * bp, 16), bp)
        r4.append(send(se.at[h2, theirs], rb.at[k - 1], (rs_s, rs_r, rs), dev(zh=h2, zl=b2 * nq + q)))
        rs += 1
    for s in r4:
        s.wait_recv()
    mine = pl.ds(pl.multiple_of(b * bp, 16), bp)
    t = se[zh, mine].astype(F32)
    for k in range(NZH * nb - 1):
        t += rb[k].astype(F32)
    ox[x, q, mine] = t.astype(BF)

    for ref, peer_ids in (
        (ox.at[x, q, mine], [dev(zl=((b + k) % nb) * nq + q) for k in range(1, nb)]),
        (ox.at[x, q], [dev(zl=b * nq + (q + k) % nq) for k in range(1, nq)]),
        (ox.at[x], [dev(x=(x + k) % nx) for k in range(1, nx)]),
    ):
        step = []
        for p in peer_ids:
            step.append(send(ref, ref, (rs_s, rs_r, rs), p))
            rs += 1
        for s in step:
            s.wait_recv()

    for s in a2:
        s.wait_recv()
    owned_ref[...] = av4[...]
    scale = 1.0 / (nx * nzl * NF)

    def unit(i):
        at = i * 16
        px, at = at // xp, at % xp
        return ox[px, at // qp, at % qp : at % qp + 16, :].astype(F32) * scale

    for i in range(16):
        gdn_ref[16 * i : 16 * i + 16, 0:128] = unit(i)
        gdn_ref[16 * i : 16 * i + 16, 128:256] = unit(16 + i)
        t = unit(32 + i)
        gup_ref[:, 256 * i : 256 * i + 128] = t[0:8]
        gup_ref[:, 256 * i + 128 : 256 * i + 256] = t[8:16]
    gproj_ref[...] = unit(48)
    for s in pending:
        s.wait_send()


def per_device(split, embeddings, cotangent, owners, projection, up_weight, down_weight):
    nx, nzl, nq = split
    nb = nzl // nq
    feats, width = embeddings.shape[1:]
    units = ROWS // 16
    xu = -(-units // nx)
    bu = -(-xu // (nq * nb))
    xp, bp = 16 * xu, 16 * bu
    qp = nb * bp
    n_ag = 6 + (nq - 1) + (nx - 1) + 4 + 6
    n_rs = 2 + 3 + (nx - 1) * 2 + (nq - 1) * 2 + (NZH * nb - 1) + (nb - 1)
    n_aa = nzl - 1 + nx - 1
    vmem = pl.BlockSpec(memory_space=pltpu.VMEM)
    return pl.pallas_call(
        functools.partial(kernel, split),
        out_shape=(
            jax.ShapeDtypeStruct((feats, width), BF),
            jax.ShapeDtypeStruct(projection.shape, F32),
            jax.ShapeDtypeStruct(up_weight.shape, F32),
            jax.ShapeDtypeStruct(down_weight.shape, F32),
        ),
        in_specs=[vmem] * 6,
        out_specs=(vmem,) * 4,
        scratch_shapes=[
            pltpu.VMEM((NF, ROWS, 128), BF),
            pltpu.VMEM((NZH, NY, NC, ROWS, 128), BF),
            pltpu.VMEM((NZH, NY, ROWS, 128), BF),
            pltpu.VMEM((NY, NZH, ROWS, 128), BF),
            pltpu.VMEM((NY - 1, NZH, ROWS, 128), BF),
            pltpu.VMEM((NZH, nx * xp, 128), BF),
            pltpu.VMEM((nx - 1, NZH, xp, 128), BF),
            pltpu.VMEM((NZH, nq * qp, 128), BF),
            pltpu.VMEM((nq - 1, NZH, qp, 128), BF),
            pltpu.VMEM((NZH, qp, 128), BF),
            pltpu.VMEM((NZH * nb - 1, bp, 128), BF),
            pltpu.VMEM((nx, nq, qp, 128), BF),
            pltpu.VMEM((feats, 128), BF),
            pltpu.VMEM((feats, 128), F32),
            pltpu.VMEM((feats, width), BF),
            pltpu.VMEM((feats, width), BF),
            pltpu.VMEM((feats, width), BF),
            pltpu.VMEM((feats, width), BF),
            pltpu.SemaphoreType.DMA((n_ag,)),
            pltpu.SemaphoreType.DMA((n_ag,)),
            pltpu.SemaphoreType.DMA((n_rs,)),
            pltpu.SemaphoreType.DMA((n_rs,)),
            pltpu.SemaphoreType.DMA((n_aa,)),
            pltpu.SemaphoreType.DMA((n_aa,)),
        ],
        compiler_params=pltpu.CompilerParams(
            collective_id=0, has_side_effects=True, vmem_limit_bytes=48 * 1024 * 1024
        ),
        name="layer_backward",
    )(embeddings, cotangent, owners, projection, up_weight, down_weight)


def solution(mesh):
    return jax.shard_map(
        functools.partial(per_device, SPLITS[mesh.shape["dp"]]),
        mesh=mesh,
        in_specs=(
            P(("dp", "fsdp"), None, None),
            P(("dp", "fsdp"), None, None),
            P(("dp", "fsdp"), None),
            P("fsdp", None),
            P("fsdp", None),
            P("fsdp", None),
        ),
        out_specs=(P(("dp", "fsdp"), None), P("fsdp", None), P("fsdp", None), P("fsdp", None)),
        check_vma=False,
    )
```

time: 1500 us -> 135 us (0.09)
  blocking collectives: 822 us -> 0 us
  waiting for transfers between devices: 629 us -> 0 us
  Pallas kernels: 0 us -> 126 us
  matrix products: 18.9 us -> 0 us
    psum x1 -> x0, blocking collectives: 762 us -> none  [per_device(): lax.psum((share_proj, share_up, share_down), 'dp')]
    reduce_scatter x2 -> x0, waiting for transfers between devices: 326 us -> none  [the longest x1 177 us: per_device(): lax.psum_scatter(part_down.astype(jnp.bfloat16), 'fsdp', scatter_dimensio...]
    all_gather x2 -> x0, waiting for transfers between devices: 203 us -> none  [the longest x1 132 us: per_device(): lax.all_gather(down_weight, 'fsdp', axis=0, tiled=True)]
    pallas_call x0 -> x1, Pallas kernels: none -> 126 us  [per_device(): pl.pallas_call(functools.partial(kernel, split), out_shape=(jax.ShapeDtyp...]
    unnamed x6 -> x0, waiting for transfers between devices: 101 us -> none
    all_gather x1 -> x0, blocking collectives: 59.2 us -> none  [per_device(): lax.all_gather(projection, 'fsdp', axis=0, tiled=True)]
    dot_general x11 -> x0, matrix products: 18.9 us -> none  [the longest x1 5.1 us: local_backward(): jnp.einsum('rh,rd->hd', activated, cot_rows, preferred_element_type=jnp.f...]
  transfers between devices with their start and end apart: 6 -> 0, of which waited for: 5 -> 0; matrix products, arithmetic and copies ran while one was open for 1% -> 0% of each run, Pallas kernels for 0% -> 0%
where the time goes in v1:
time: 135 us; the launch traced here: 134 us
  Pallas kernels  126 us (93%)
  local copies, waits for them, and re-layouts  7.52 us (6%)
    pallas_call x1, Pallas kernels, per_device(): pl.pallas_call(functools.partial(kernel, split), out_shape=(jax.ShapeDtyp...  126 us
    unnamed x16, local copies, waits for them, and re-layouts  7.52 us

profile of v1, /device:TPU:24, one launch (start us, length us, event | category | flops | bytes accessed | tf_op | source)
XLA Modules:
  0.0 134.2 jit_solution(3606356588700202723)
XLA Ops:
  0.6 0.0 copy-start
  0.6 0.9 copy-done
  1.5 0.0 copy-start.1
  1.5 0.9 copy-done.1
  2.4 0.0 copy-start.2
  2.4 0.9 copy-done.2
  3.3 0.0 copy-start.3
  3.3 0.8 copy-done.3
  4.2 0.0 copy-start.4
  4.2 0.7 copy-done.4
  4.9 0.0 copy-start.5
  4.9 0.7 copy-done.5
  5.6 126.1 %layer_backward.1 = (bf16[256,256]{1,0:T(8,128)(2,1)S(1)}, f32[16,128]{1,0:T(8,128)S(1)}, f32[8,4096]{1,0:T(8,128)S(1)}, f32[256,256]{1,0:T(8,128)S(1)}) custom-call(bf16[1,256,256]{2,1,0:T(8,128)(2,1)S(1)} %copy-done, bf16[1,256,256]{2,1,0:T(8,128)(2,1)S(1)} %copy-done.1, s32[1,256]{1,0:T(1,128)S(1)} %copy-done.5, bf16[16,128]{1,0:T(8,128)(2,1)S(1)} %copy-done.4, ...), custom_call_target="tpu_custom_call" | custom-call | tf_op jit(solution)/shard_map/layer_backward/pallas_call | solution.py:328
  131.6 0.7 copy.14
  132.3 0.6 copy.15
  132.9 0.7 copy.16
  133.5 0.7 copy.17
Async XLA Ops:
  0.6 0.9 copy-start
  1.5 0.9 copy-start.1
  2.4 0.9 copy-start.2
  3.3 0.8 copy-start.3
  4.2 0.7 copy-start.4
  4.9 0.7 copy-start.5

commit v2 on v1

v2 whole, which is shorter than its diff:
```python
import functools

import jax
import jax.numpy as jnp
from jax import lax
from jax.experimental import pallas as pl
from jax.experimental.pallas import tpu as pltpu
from jax.sharding import PartitionSpec as P

BF = jnp.bfloat16
F32 = jnp.float32
SPLITS = {64: (4, 16, 4), 4: (2, 2, 2), 8: (2, 4, 2)}
NZH, NY, NC = 2, 4, 2
NF = NZH * NY * NC
MAIN, ROWS, CUT = 768, 784, 384


def mm(a, b, ca=1, cb=0):
    return lax.dot_general(a, b, (((ca,), (cb,)), ((), ())), preferred_element_type=F32)


def kernel(
    split, x_hbm, cot_hbm, own_hbm, proj_hbm, up_hbm, dn_hbm,
    owned_ref, gproj_ref, gup_ref, gdn_ref,
    x_ref, cot_ref, own_ref, up_ref,
    wg, gg, rc, sa, rya, sba, rxa, rxb, sbb, ryb, sc, rq, se, rb, ox,
    nl, nlt, gn, av1, av2, av3, av4,
    in_s, ag_s, ag_r, co_s, co_r, rs_s, rs_r, aa_s, aa_r,
):
    nx, nzl, nq = split
    nb = nzl // nq
    feats = x_ref.shape[0]
    xa, xb = rxa.shape[2], rxb.shape[3]
    xp, qp = xa + xb, se.shape[1]
    zrows = feats // nzl
    per = zrows // nx
    dp, fs = lax.axis_index("dp"), lax.axis_index("fsdp")
    x, zl = dp // nzl, dp % nzl
    zh, y, c = fs // (NY * NC), (fs // NC) % NY, fs % NC
    q, b = zl % nq, zl // nq

    def dev(x=x, zl=zl, zh=zh, y=y, c=c):
        return {"dp": x * nzl + zl, "fsdp": (zh * NY + y) * NC + c}

    pending = []

    def remote(src, dst, ssem, rsem, i, to):
        return pltpu.make_async_remote_copy(
            src_ref=src, dst_ref=dst, send_sem=ssem.at[i], recv_sem=rsem.at[i],
            device_id=to, device_id_type=pl.DeviceIdType.MESH,
        )

    def sender(ssem, rsem):
        count = [0]

        def send(src, dst, to):
            copy = remote(src, dst, ssem, rsem, count[0], to)
            count[0] += 1
            copy.start()
            pending.append(copy)
            return copy

        return send

    def rows(start, size):
        return pl.ds(pl.multiple_of(start, 16), size)

    gather, reduce, exchange = sender(ag_s, ag_r), sender(rs_s, rs_r), sender(aa_s, aa_r)
    sibling = dev(c=1 - c)
    near_y = {k: dev(y=(y + k) % NY) for k in (1, 3, 2)}
    near_x = {k: dev(x=(x + k) % nx) for k in range(1, nx)}

    barrier = pltpu.get_barrier_semaphore()
    peers = [sibling]
    peers += [
        dev(x=(x + i) % nx, y=(y + k) % NY) for i in range(nx) for k in range(NY) if i or k
    ]
    peers += [dev(zl=(zl + k) % nzl) for k in range(1, nzl)]
    peers += [dev(zh=1 - zh, zl=((b + k) % nb) * nq + q) for k in range(nb)]
    half = ((zl + nzl // 2) % nzl)
    if (nzl // 2) % nq:
        peers.append(dev(zh=1 - zh, zl=half))
    for p in peers:
        pl.semaphore_signal(barrier, inc=1, device_id=p, device_id_type=pl.DeviceIdType.MESH)

    inputs = [
        pltpu.make_async_copy(src, dst, in_s.at[i])
        for i, (src, dst) in enumerate(
            (
                (up_hbm, up_ref),
                (proj_hbm, wg.at[zh, y, c, MAIN:ROWS]),
                (dn_hbm.at[:, 0:128], wg.at[zh, y, c, 0:256]),
                (dn_hbm.at[:, 128:256], wg.at[zh, y, c, 256:512]),
                (x_hbm.at[0], x_ref),
                (own_hbm, own_ref),
                (cot_hbm.at[0], cot_ref),
            )
        )
    ]
    for copy in inputs:
        copy.start()
    inputs[0].wait()
    for u in range(NF):
        lo = up_ref[:, 256 * u : 256 * u + 128].astype(F32)
        hi = up_ref[:, 256 * u + 128 : 256 * u + 256].astype(F32)
        wg[zh, y, c, 512 + 16 * u : 528 + 16 * u] = jnp.concatenate([lo, hi], axis=0).astype(BF)
    for copy in inputs[1:4]:
        copy.wait()
    pl.semaphore_wait(barrier, len(peers))

    part = MAIN // (nx * nq)
    main, tail = pl.ds(0, MAIN), pl.ds(MAIN, ROWS - MAIN)
    oz = 1 - zh
    own, other = wg.at[zh, y, c], wg.at[oz, y, c]
    far = dev(zh=oz, zl=half)
    piece = rows((x * nq + half % nq) * part, part)
    far_main = gather(own.at[piece], own.at[piece], far)
    far_tail = gather(own.at[tail], own.at[tail], far)
    tails = [gather(own.at[tail], own.at[tail], to) for to in near_y.values()]
    to_core = [gather(own.at[tail], own.at[tail], sibling)]
    mains = [gather(own.at[main], own.at[main], to) for to in near_y.values()]
    mains_core = [gather(own.at[main], own.at[main], sibling)]
    for k, copy in zip(near_y, tails):
        copy.wait_recv()
        got = wg.at[zh, (y - k + NY) % NY, c, tail]
        to_core.append(gather(got, got, sibling))
    far_main.wait_recv()
    piece = rows((x * nq + q) * part, part)
    step = [
        gather(other.at[piece], other.at[piece], dev(zl=b * nq + (q + k) % nq))
        for k in range(1, nq)
    ]
    far_tail.wait_recv()
    tails = [gather(other.at[tail], other.at[tail], to) for to in near_y.values()]
    to_core.append(gather(other.at[tail], other.at[tail], sibling))
    for s in step:
        s.wait_recv()
    piece = rows(x * nq * part, nq * part)
    shares = {}
    for i in range(nx):
        for k in (1, 3, 2, 0):
            if i or k:
                shares[i, k] = gather(
                    other.at[piece], other.at[piece], dev(x=(x + i) % nx, y=(y + k) % NY)
                )
    for k, copy in zip(near_y, tails):
        copy.wait_recv()
        got = wg.at[oz, (y - k + NY) % NY, c, tail]
        to_core.append(gather(got, got, sibling))
    for k, copy in zip(near_y, mains):
        copy.wait_recv()
        got = wg.at[zh, (y - k + NY) % NY, c, main]
        mains_core.append(gather(got, got, sibling))

    for s in to_core:
        s.wait_recv()
    inputs[4].wait()
    emb = x_ref[...]
    proj = wg[:, :, :, MAIN:ROWS, :].reshape(feats, 128)
    compressed = mm(emb, proj, 0, 0).astype(BF)
    fm = mm(emb, compressed)
    centre = fm - jnp.mean(fm, axis=-1, keepdims=True)
    inv = lax.rsqrt(jnp.mean(centre * centre, axis=-1, keepdims=True) + 1e-05)
    normed = centre * inv
    nl[...] = normed.astype(BF)
    nlt[...] = normed.T.astype(BF)
    gn[...] = jnp.zeros_like(gn)
    inputs[5].wait()
    inputs[6].wait()

    for i in range(nx):
        for k in range(NY):
            if i or k:
                shares[i, k].wait_recv()
        got = wg.at[oz, :, c, rows(((x - i + nx) % nx) * nq * part, nq * part)]
        mains_core.append(gather(got, got, sibling))
    for s in mains_core:
        s.wait_recv()

    def hidden_units(izh, iy, ic):
        u = (izh * NY + iy) * NC + ic
        urows = rows(512 + 16 * u, 16)
        pieces = wg[:, :, :, urows, :].reshape(NF, 16, 128).astype(F32)
        up = jnp.concatenate(
            [pieces[:, 0:8].reshape(128, 128), pieces[:, 8:16].reshape(128, 128)], axis=1
        ).astype(BF)
        down = jnp.concatenate([wg[izh, iy, ic, 0:256], wg[izh, iy, ic, 256:512]], axis=1)
        cots = cot_ref[...]
        hidden = mm(nl[...], up)
        sig = 0.5 * jnp.tanh(0.5 * hidden) + 0.5
        act = (hidden * sig).astype(BF)
        gh = (mm(cots, down, 1, 1) * sig * (1.0 + hidden * (1.0 - sig))).astype(BF)
        gn[...] += mm(gh, up, 1, 1)
        gup = mm(nlt[...], gh)
        gup = jnp.concatenate(
            [gup[:, 0:128].reshape(NF, 8, 128), gup[:, 128:256].reshape(NF, 8, 128)], axis=1
        ).astype(BF)
        gg[:, :, :, urows, :] = gup.reshape(NZH, NY, NC, 16, 128)
        gdn = mm(act, cots, 0, 0).astype(BF)
        gg[izh, iy, ic, 0:256] = gdn[:, 0:128]
        gg[izh, iy, ic, 256:512] = gdn[:, 128:256]

    def core_copy(i):
        izh, iy = i // NY, i % NY
        down = pl.ds(0, 512)
        return remote(
            gg.at[izh, iy, 1 - c, down], rc.at[izh, iy, down], co_s, co_r, i, sibling
        )

    @pl.loop(0, NZH * NY)
    def _(i):
        hidden_units(i // NY, i % NY, 1 - c)
        core_copy(i).start()
        hidden_units(i // NY, i % NY, c)

    upper = pl.ds(512, MAIN - 512)
    r0 = [reduce(gg.at[:, :, 1 - c, upper], rc.at[:, :, upper], sibling)]
    for i in range(NZH * NY):
        core_copy(i).wait()
    r1a = []
    blk = 96
    for k in (1, 3, 2, 0):
        to = (y + k) % NY

        @pl.loop(0, CUT // blk)
        def _(i, to=to):
            r = rows(i * blk, blk)
            sa[to, :, r] = (gg[:, to, c, r].astype(F32) + rc[:, to, r].astype(F32)).astype(BF)

        if k:
            r1a.append(reduce(sa.at[to, :, 0:CUT], rya.at[k - 1], near_y[k]))

    gnorm = gn[...]
    gfm = inv * (
        gnorm
        - jnp.mean(gnorm, axis=-1, keepdims=True)
        - normed * jnp.mean(gnorm * normed, axis=-1, keepdims=True)
    )
    gfm = gfm.astype(BF)
    gcomp = mm(emb, gfm, 0, 0).astype(BF)
    gproj = mm(emb, gcomp).astype(BF)
    gg[:, :, :, MAIN:ROWS, :] = gproj.reshape(NZH, NY, NC, 16, 128)
    r0.append(reduce(gg.at[:, :, 1 - c, tail], rc.at[:, :, tail], sibling))
    for s in r0:
        s.wait_recv()
    r1b = []
    for k in [*range(1, nx), 0]:
        at = rows(CUT + ((x + k) % nx) * xb, xb)

        @pl.loop(0, NY)
        def _(i, at=at):
            sa[i, :, at] = (gg[:, i, c, at].astype(F32) + rc[:, i, at].astype(F32)).astype(BF)

        if k:
            r1b.append(reduce(sa.at[:, :, at], rxb.at[k - 1], near_x[k]))

    gemb = (mm(gfm, compressed, 1, 1) + mm(proj, gcomp, 1, 1)).astype(BF)

    row = lax.broadcasted_iota(jnp.int32, (feats, feats), 0)
    col = lax.broadcasted_iota(jnp.int32, (feats, feats), 1)
    across_f = jnp.broadcast_to(own_ref[...].astype(F32), (feats, feats))
    down_f = jnp.sum(jnp.where(row == col, across_f, 0.0), axis=1, keepdims=True)
    within = jnp.sum(
        jnp.where((across_f == down_f) & (row < col), 1.0, 0.0), axis=0, keepdims=True
    )
    owner = across_f[0:1]
    owner_x = jnp.floor(owner * (1.0 / nzl))
    place = (owner - owner_x * nzl) * zrows + owner_x * per + within
    perm = jnp.where(row.astype(F32) == place, 1.0, 0.0).astype(BF)
    av1[...] = mm(perm, gemb).astype(BF)
    a1 = []
    mine = rows(zl * zrows, zrows)
    for k in range(1, nzl):
        to = (zl + k) % nzl
        a1.append(exchange(av1.at[rows(to * zrows, zrows)], av2.at[mine], dev(zl=to)))
    av2[mine] = av1[mine]

    for s in r1a:
        s.wait_recv()
    r2 = []
    for k in [*range(1, nx), 0]:
        at = rows(((x + k) % nx) * xa, xa)
        t = sa[y, :, at].astype(F32)
        for j in range(NY - 1):
            t += rya[j, :, at].astype(F32)
        sba[:, at] = t.astype(BF)
        if k:
            r2.append(reduce(sba.at[:, at], rxa.at[k - 1], near_x[k]))
    for s in r1b:
        s.wait_recv()
    at = rows(CUT + x * xb, xb)
    for k in (1, 3, 2, 0):
        to = (y + k) % NY
        t = sa[to, :, at].astype(F32)
        for j in range(nx - 1):
            t += rxb[j, to].astype(F32)
        sbb[to] = t.astype(BF)
        if k:
            r2.append(reduce(sbb.at[to], ryb.at[k - 1], near_y[k]))
    for s in r2:
        s.wait_recv()
    t = sba[:, rows(x * xa, xa)].astype(F32)
    for j in range(nx - 1):
        t += rxa[j].astype(F32)
    sc[:, 0:xa] = t.astype(BF)
    t = sbb[y].astype(F32)
    for j in range(NY - 1):
        t += ryb[j].astype(F32)
    sc[:, xa:xp] = t.astype(BF)

    r3 = []
    for k in range(1, nq):
        to = (q + k) % nq
        r3.append(reduce(sc.at[:, rows(to * qp, qp)], rq.at[k - 1], dev(zl=b * nq + to)))
    for s in r3:
        s.wait_recv()
    t = sc[:, rows(q * qp, qp)].astype(F32)
    for j in range(nq - 1):
        t += rq[j].astype(F32)
    se[...] = t.astype(BF)

    r4 = []
    for k in range(NZH * nb - 1, 0, -1):
        h2, b2 = (zh + k // nb) % NZH, (b + k % nb) % nb
        r4.append(reduce(se.at[h2], rb.at[k - 1], dev(zh=h2, zl=b2 * nq + q)))

    for s in a1:
        s.wait_recv()
    r_z, r_x, r_k = col // zrows, (col % zrows) // per, col % per
    perm = jnp.where(row == r_x * (nzl * per) + r_z * per + r_k, 1.0, 0.0).astype(BF)
    av3[...] = mm(perm, av2[...]).astype(BF)
    a2 = []
    xrows = nzl * per
    mine = rows(x * xrows, xrows)
    for k in range(1, nx):
        to = (x + k) % nx
        a2.append(exchange(av3.at[rows(to * xrows, xrows)], av4.at[mine], near_x[k]))
    av4[mine] = av3[mine]

    for s in r4:
        s.wait_recv()
    t = se[zh].astype(F32)
    for j in range(NZH * nb - 1):
        t += rb[j].astype(F32)
    mine = rows(q * qp, qp)
    ox[x, mine] = t.astype(BF)

    ref = ox.at[x, mine]
    step = [reduce(ref, ref, dev(zl=b * nq + (q + k) % nq)) for k in range(1, nq)]
    for s in a2:
        s.wait_recv()
    owned_ref[...] = av4[...]
    for s in step:
        s.wait_recv()
    ref = ox.at[x, 0:xp]
    step = [reduce(ref, ref, to) for to in near_x.values()]
    for s in step:
        s.wait_recv()

    scale = 1.0 / (nx * nzl * NF)

    def unit(i):
        at = i * 16
        px, at = (at // xa, at % xa) if at < CUT else ((at - CUT) // xb, xa + (at - CUT) % xb)
        return ox[px, at : at + 16, :].astype(F32) * scale

    for i in range(16):
        gdn_ref[16 * i : 16 * i + 16, 0:128] = unit(i)
        gdn_ref[16 * i : 16 * i + 16, 128:256] = unit(16 + i)
        t = unit(32 + i)
        gup_ref[:, 256 * i : 256 * i + 128] = t[0:8]
        gup_ref[:, 256 * i + 128 : 256 * i + 256] = t[8:16]
    gproj_ref[...] = unit(48)
    for s in pending:
        s.wait_send()


def per_device(split, embeddings, cotangent, owners, projection, up_weight, down_weight):
    nx, nzl, nq = split
    nb = nzl // nq
    feats, width = embeddings.shape[1:]
    xa = CUT // nx
    xb = 16 * -(-(ROWS - CUT) // (16 * nx))
    qp = 16 * -(-(xa + xb) // (16 * nq))
    padded = CUT + nx * xb
    n_ag = 20 + (nq - 1) + (nx * NY - 1) + 3 + nx
    n_rs = 2 + 2 * (NY - 1) + 3 * (nx - 1) + 2 * (nq - 1) + (NZH * nb - 1)
    n_aa = nzl - 1 + nx - 1
    vmem = pl.BlockSpec(memory_space=pltpu.VMEM)
    return pl.pallas_call(
        functools.partial(kernel, split),
        out_shape=(
            jax.ShapeDtypeStruct((feats, width), BF),
            jax.ShapeDtypeStruct(projection.shape, F32),
            jax.ShapeDtypeStruct(up_weight.shape, F32),
            jax.ShapeDtypeStruct(down_weight.shape, F32),
        ),
        in_specs=[pl.BlockSpec(memory_space=pl.ANY)] * 6,
        out_specs=(vmem,) * 4,
        scratch_shapes=[
            pltpu.VMEM((feats, width), BF),
            pltpu.VMEM((feats, width), BF),
            pltpu.VMEM(owners.shape, jnp.int32),
            pltpu.VMEM(up_weight.shape, BF),
            pltpu.VMEM((NZH, NY, NC, ROWS, 128), BF),
            pltpu.VMEM((NZH, NY, NC, padded, 128), BF),
            pltpu.VMEM((NZH, NY, padded, 128), BF),
            pltpu.VMEM((NY, NZH, padded, 128), BF),
            pltpu.VMEM((NY - 1, NZH, CUT, 128), BF),
            pltpu.VMEM((NZH, CUT, 128), BF),
            pltpu.VMEM((nx - 1, NZH, xa, 128), BF),
            pltpu.VMEM((nx - 1, NY, NZH, xb, 128), BF),
            pltpu.VMEM((NY, NZH, xb, 128), BF),
            pltpu.VMEM((NY - 1, NZH, xb, 128), BF),
            pltpu.VMEM((NZH, nq * qp, 128), BF),
            pltpu.VMEM((nq - 1, NZH, qp, 128), BF),
            pltpu.VMEM((NZH, qp, 128), BF),
            pltpu.VMEM((NZH * nb - 1, qp, 128), BF),
            pltpu.VMEM((nx, nq * qp, 128), BF),
            pltpu.VMEM((feats, 128), BF),
            pltpu.VMEM((128, feats), BF),
            pltpu.VMEM((feats, 128), F32),
            pltpu.VMEM((feats, width), BF),
            pltpu.VMEM((feats, width), BF),
            pltpu.VMEM((feats, width), BF),
            pltpu.VMEM((feats, width), BF),
            pltpu.SemaphoreType.DMA((7,)),
            pltpu.SemaphoreType.DMA((n_ag,)),
            pltpu.SemaphoreType.DMA((n_ag,)),
            pltpu.SemaphoreType.DMA((NZH * NY,)),
            pltpu.SemaphoreType.DMA((NZH * NY,)),
            pltpu.SemaphoreType.DMA((n_rs,)),
            pltpu.SemaphoreType.DMA((n_rs,)),
            pltpu.SemaphoreType.DMA((n_aa,)),
            pltpu.SemaphoreType.DMA((n_aa,)),
        ],
        compiler_params=pltpu.CompilerParams(
            collective_id=0, has_side_effects=True, vmem_limit_bytes=48 * 1024 * 1024
        ),
        name="layer_backward",
    )(embeddings, cotangent, owners, projection, up_weight, down_weight)


def solution(mesh):
    return jax.shard_map(
        functools.partial(per_device, SPLITS[mesh.shape["dp"]]),
        mesh=mesh,
        in_specs=(
            P(("dp", "fsdp"), None, None),
            P(("dp", "fsdp"), None, None),
            P(("dp", "fsdp"), None),
            P("fsdp", None),
            P("fsdp", None),
            P("fsdp", None),
        ),
        out_specs=(P(("dp", "fsdp"), None), P("fsdp", None), P("fsdp", None), P("fsdp", None)),
        check_vma=False,
    )
```

time: 135 us -> 119 us (0.88)
  Pallas kernels: 126 us -> 110 us
    pallas_call x1, Pallas kernels: 126 us -> 110 us  [per_device(): pl.pallas_call(functools.partial(kernel, split), out_shape=(jax.ShapeDtyp...]
where the time goes in v2:
time: 119 us; the launch traced here: 118 us
  Pallas kernels  110 us (92%)
  local copies, waits for them, and re-layouts  7.52 us (6%)
    pallas_call x1, Pallas kernels, per_device(): pl.pallas_call(functools.partial(kernel, split), out_shape=(jax.ShapeDtyp...  110 us
    unnamed x16, local copies, waits for them, and re-layouts  7.52 us

profile of v2, /device:TPU:24, one launch (start us, length us, event | category | flops | bytes accessed | tf_op | source)
XLA Modules:
  0.0 118.4 jit_solution(1527289466032830492)
XLA Ops:
  0.6 0.0 copy-start
  0.6 0.9 copy-done
  1.5 0.0 copy-start.1
  1.5 0.9 copy-done.1
  2.4 0.0 copy-start.2
  2.4 0.9 copy-done.2
  3.3 0.0 copy-start.3
  3.3 0.8 copy-done.3
  4.2 0.0 copy-start.4
  4.2 0.7 copy-done.4
  4.9 0.0 copy-start.5
  4.9 0.7 copy-done.5
  5.6 110.2 %layer_backward.1 = (bf16[256,256]{1,0:T(8,128)(2,1)S(1)}, f32[16,128]{1,0:T(8,128)S(1)}, f32[8,4096]{1,0:T(8,128)S(1)}, f32[256,256]{1,0:T(8,128)S(1)}) custom-call(bf16[1,256,256]{2,1,0:T(8,128)(2,1)S(1)} %copy-done, bf16[1,256,256]{2,1,0:T(8,128)(2,1)S(1)} %copy-done.1, s32[1,256]{1,0:T(1,128)S(1)} %copy-done.5, bf16[16,128]{1,0:T(8,128)(2,1)S(1)} %copy-done.4, ...), custom_call_target="tpu_custom_call" | custom-call | tf_op jit(solution)/shard_map/layer_backward/pallas_call | solution.py:390
  115.8 0.7 copy.14
  116.4 0.6 copy.15
  117.0 0.7 copy.16
  117.7 0.7 copy.17
Async XLA Ops:
  0.6 0.9 copy-start
  1.5 0.9 copy-start.1
  2.4 0.9 copy-start.2
  3.3 0.8 copy-start.3
  4.2 0.7 copy-start.4
  4.9 0.7 copy-start.5

commit v3 on v2

--- a/solution.py
+++ b/solution.py
@@ -12,7 +12,7 @@
 SPLITS = {64: (4, 16, 4), 4: (2, 2, 2), 8: (2, 4, 2)}
 NZH, NY, NC = 2, 4, 2
 NF = NZH * NY * NC
-MAIN, ROWS, CUT = 768, 784, 384
+MAIN, ROWS, CUT = 768, 784, 512
 
 
 def mm(a, b, ca=1, cb=0):
@@ -23,7 +23,7 @@
     split, x_hbm, cot_hbm, own_hbm, proj_hbm, up_hbm, dn_hbm,
     owned_ref, gproj_ref, gup_ref, gdn_ref,
     x_ref, cot_ref, own_ref, up_ref,
-    wg, gg, rc, sa, rya, sba, rxa, rxb, sbb, ryb, sc, rq, se, rb, ox,
+    wg, gg, rc, sa, rya, sba, rxa, rxb, sbb, ryb, ryt, st, rxt, sc, rq, se, rb, ox,
     nl, nlt, gn, av1, av2, av3, av4,
     in_s, ag_s, ag_r, co_s, co_r, rs_s, rs_r, aa_s, aa_r,
 ):
@@ -32,6 +32,7 @@
     feats = x_ref.shape[0]
     xa, xb = rxa.shape[2], rxb.shape[3]
     xp, qp = xa + xb, se.shape[1]
+    pq = xp // nq
     zrows = feats // nzl
     per = zrows // nx
     dp, fs = lax.axis_index("dp"), lax.axis_index("fsdp")
@@ -108,49 +109,63 @@
         copy.wait()
     pl.semaphore_wait(barrier, len(peers))
 
-    part = MAIN // (nx * nq)
+    parts = ((CUT, (MAIN - CUT) // (nx * nq)), (0, CUT // (nx * nq)))
     main, tail = pl.ds(0, MAIN), pl.ds(MAIN, ROWS - MAIN)
     oz = 1 - zh
     own, other = wg.at[zh, y, c], wg.at[oz, y, c]
     far = dev(zh=oz, zl=half)
-    piece = rows((x * nq + half % nq) * part, part)
-    far_main = gather(own.at[piece], own.at[piece], far)
-    far_tail = gather(own.at[tail], own.at[tail], far)
-    tails = [gather(own.at[tail], own.at[tail], to) for to in near_y.values()]
-    to_core = [gather(own.at[tail], own.at[tail], sibling)]
-    mains = [gather(own.at[main], own.at[main], to) for to in near_y.values()]
-    mains_core = [gather(own.at[main], own.at[main], sibling)]
+
+    def swap(ref, to):
+        return gather(ref, ref, to)
+
+    far_main = []
+    for base, size in parts:
+        far_main.append(swap(own.at[rows(base + (x * nq + half % nq) * size, size)], far))
+        if base:
+            far_tail = swap(own.at[tail], far)
+    tails = [swap(own.at[tail], to) for to in near_y.values()]
+    to_core = [swap(own.at[tail], sibling)]
+    mains = [swap(own.at[main], to) for to in near_y.values()]
+    mains_core = [swap(own.at[main], sibling)]
     for k, copy in zip(near_y, tails):
         copy.wait_recv()
-        got = wg.at[zh, (y - k + NY) % NY, c, tail]
-        to_core.append(gather(got, got, sibling))
-    far_main.wait_recv()
-    piece = rows((x * nq + q) * part, part)
-    step = [
-        gather(other.at[piece], other.at[piece], dev(zl=b * nq + (q + k) % nq))
-        for k in range(1, nq)
-    ]
-    far_tail.wait_recv()
-    tails = [gather(other.at[tail], other.at[tail], to) for to in near_y.values()]
-    to_core.append(gather(other.at[tail], other.at[tail], sibling))
-    for s in step:
-        s.wait_recv()
-    piece = rows(x * nq * part, nq * part)
+        to_core.append(swap(wg.at[zh, (y - k + NY) % NY, c, tail], sibling))
+    steps = []
+    for n, (base, size) in enumerate(parts):
+        far_main[n].wait_recv()
+        piece = rows(base + (x * nq + q) * size, size)
+        steps.append(
+            [swap(other.at[piece], dev(zl=b * nq + (q + k) % nq)) for k in range(1, nq)]
+        )
+        if n == 0:
+            far_tail.wait_recv()
+            tails = [swap(other.at[tail], to) for to in near_y.values()]
+            to_core.append(swap(other.at[tail], sibling))
     shares = {}
-    for i in range(nx):
-        for k in (1, 3, 2, 0):
-            if i or k:
-                shares[i, k] = gather(
-                    other.at[piece], other.at[piece], dev(x=(x + i) % nx, y=(y + k) % NY)
-                )
+    for n, (base, size) in enumerate(parts):
+        for s in steps[n]:
+            s.wait_recv()
+        piece = rows(base + x * nq * size, nq * size)
+        for i in range(nx):
+            for k in (1, 3, 2, 0):
+                if i or k:
+                    shares[n, i, k] = swap(
+                        other.at[piece], dev(x=(x + i) % nx, y=(y + k) % NY)
+                    )
     for k, copy in zip(near_y, tails):
         copy.wait_recv()
-        got = wg.at[oz, (y - k + NY) % NY, c, tail]
-        to_core.append(gather(got, got, sibling))
+        to_core.append(swap(wg.at[oz, (y - k + NY) % NY, c, tail], sibling))
     for k, copy in zip(near_y, mains):
         copy.wait_recv()
-        got = wg.at[zh, (y - k + NY) % NY, c, main]
-        mains_core.append(gather(got, got, sibling))
+        mains_core.append(swap(wg.at[zh, (y - k + NY) % NY, c, main], sibling))
+
+    def to_sibling(n, i):
+        base, size = parts[n]
+        for k in range(NY):
+            if i or k:
+                shares[n, i, k].wait_recv()
+        at = rows(base + ((x - i + nx) % nx) * nq * size, nq * size)
+        return swap(wg.at[oz, :, c, at], sibling)
 
     for s in to_core:
         s.wait_recv()
@@ -168,12 +183,7 @@
     inputs[5].wait()
     inputs[6].wait()
 
-    for i in range(nx):
-        for k in range(NY):
-            if i or k:
-                shares[i, k].wait_recv()
-        got = wg.at[oz, :, c, rows(((x - i + nx) % nx) * nq * part, nq * part)]
-        mains_core.append(gather(got, got, sibling))
+    mains_core += [to_sibling(0, i) for i in range(nx)]
     for s in mains_core:
         s.wait_recv()
 
@@ -200,35 +210,63 @@
         gg[izh, iy, ic, 0:256] = gdn[:, 0:128]
         gg[izh, iy, ic, 256:512] = gdn[:, 128:256]
 
-    def core_copy(i):
-        izh, iy = i // NY, i % NY
-        down = pl.ds(0, 512)
+    down = pl.ds(0, CUT)
+
+    def core_copy(h, i):
+        izh = (zh + h) % NZH
         return remote(
-            gg.at[izh, iy, 1 - c, down], rc.at[izh, iy, down], co_s, co_r, i, sibling
+            gg.at[izh, i, 1 - c, down], rc.at[izh, i, down], co_s, co_r, h * NY + i, sibling
         )
 
-    @pl.loop(0, NZH * NY)
-    def _(i):
-        hidden_units(i // NY, i % NY, 1 - c)
-        core_copy(i).start()
-        hidden_units(i // NY, i % NY, c)
-
-    upper = pl.ds(512, MAIN - 512)
-    r0 = [reduce(gg.at[:, :, 1 - c, upper], rc.at[:, :, upper], sibling)]
-    for i in range(NZH * NY):
-        core_copy(i).wait()
+    def hidden_loop(h, first, last):
+        @pl.loop(first, last)
+        def _(i):
+            izh = (zh + h) % NZH
+            hidden_units(izh, i, 1 - c)
+            core_copy(h, i).start()
+            hidden_units(izh, i, c)
+
     r1a = []
-    blk = 96
-    for k in (1, 3, 2, 0):
-        to = (y + k) % NY
-
-        @pl.loop(0, CUT // blk)
-        def _(i, to=to):
-            r = rows(i * blk, blk)
-            sa[to, :, r] = (gg[:, to, c, r].astype(F32) + rc[:, to, r].astype(F32)).astype(BF)
+
+    def down_sums(h):
+        izh = (zh + h) % NZH
+        for i in range(NY):
+            core_copy(h, i).wait()
+        for k in (1, 3, 2, 0):
+            to = (y + k) % NY
+
+            @pl.loop(0, CUT // 128)
+            def _(i, to=to):
+                r = rows(i * 128, 128)
+                sa[to, izh, r] = (
+                    gg[izh, to, c, r].astype(F32) + rc[izh, to, r].astype(F32)
+                ).astype(BF)
+
+            if k:
+                r1a.append(reduce(sa.at[to, izh, down], rya.at[k - 1, izh], near_y[k]))
+
+    hidden_loop(0, 0, 2)
+    late = [to_sibling(1, i) for i in range(nx // 2)]
+    hidden_loop(0, 2, NY)
+    late += [to_sibling(1, i) for i in range(nx // 2, nx)]
+    down_sums(0)
+    for s in late:
+        s.wait_recv()
+    hidden_loop(1, 0, NY)
+    upper = pl.ds(CUT, MAIN - CUT)
+    r0 = reduce(gg.at[:, :, 1 - c, upper], rc.at[:, :, upper], sibling)
+    down_sums(1)
+    r0.wait_recv()
+    r1b = []
+    for k in [*range(1, nx), 0]:
+        at = rows(CUT + ((x + k) % nx) * xb, xb)
+
+        @pl.loop(0, NY)
+        def _(i, at=at):
+            sa[i, :, at] = (gg[:, i, c, at].astype(F32) + rc[:, i, at].astype(F32)).astype(BF)
 
         if k:
-            r1a.append(reduce(sa.at[to, :, 0:CUT], rya.at[k - 1], near_y[k]))
+            r1b.append(reduce(sa.at[:, :, at], rxb.at[k - 1], near_x[k]))
 
     gnorm = gn[...]
     gfm = inv * (
@@ -240,20 +278,7 @@
     gcomp = mm(emb, gfm, 0, 0).astype(BF)
     gproj = mm(emb, gcomp).astype(BF)
     gg[:, :, :, MAIN:ROWS, :] = gproj.reshape(NZH, NY, NC, 16, 128)
-    r0.append(reduce(gg.at[:, :, 1 - c, tail], rc.at[:, :, tail], sibling))
-    for s in r0:
-        s.wait_recv()
-    r1b = []
-    for k in [*range(1, nx), 0]:
-        at = rows(CUT + ((x + k) % nx) * xb, xb)
-
-        @pl.loop(0, NY)
-        def _(i, at=at):
-            sa[i, :, at] = (gg[:, i, c, at].astype(F32) + rc[:, i, at].astype(F32)).astype(BF)
-
-        if k:
-            r1b.append(reduce(sa.at[:, :, at], rxb.at[k - 1], near_x[k]))
-
+    r0 = reduce(gg.at[:, :, 1 - c, tail], rc.at[:, :, tail], sibling)
     gemb = (mm(gfm, compressed, 1, 1) + mm(proj, gcomp, 1, 1)).astype(BF)
 
     row = lax.broadcasted_iota(jnp.int32, (feats, feats), 0)
@@ -275,6 +300,14 @@
         a1.append(exchange(av1.at[rows(to * zrows, zrows)], av2.at[mine], dev(zl=to)))
     av2[mine] = av1[mine]
 
+    r0.wait_recv()
+    r1t = []
+    for k in (1, 3, 2, 0):
+        to = (y + k) % NY
+        sa[to, :, tail] = (gg[:, to, c, tail].astype(F32) + rc[:, to, tail].astype(F32)).astype(BF)
+        if k:
+            r1t.append(reduce(sa.at[to, :, tail], ryt.at[k - 1], near_y[k]))
+
     for s in r1a:
         s.wait_recv()
     r2 = []
@@ -297,24 +330,35 @@
         sbb[to] = t.astype(BF)
         if k:
             r2.append(reduce(sbb.at[to], ryb.at[k - 1], near_y[k]))
+    for s in r1t:
+        s.wait_recv()
+    t = sa[y, :, tail].astype(F32)
+    for j in range(NY - 1):
+        t += ryt[j].astype(F32)
+    st[...] = t.astype(BF)
+    r2 += [reduce(st, rxt.at[k - 1], near_x[k]) for k in range(1, nx)]
     for s in r2:
         s.wait_recv()
-    t = sba[:, rows(x * xa, xa)].astype(F32)
+    ta = sba[:, rows(x * xa, xa)].astype(F32)
     for j in range(nx - 1):
-        t += rxa[j].astype(F32)
-    sc[:, 0:xa] = t.astype(BF)
-    t = sbb[y].astype(F32)
+        ta += rxa[j].astype(F32)
+    tb = sbb[y].astype(F32)
     for j in range(NY - 1):
-        t += ryb[j].astype(F32)
-    sc[:, xa:xp] = t.astype(BF)
+        tb += ryb[j].astype(F32)
+    tt = st[...].astype(F32)
+    for j in range(nx - 1):
+        tt += rxt[j].astype(F32)
+    t = jnp.concatenate([ta, tb], axis=1)
+    for j in range(nq):
+        sc[:, j] = jnp.concatenate([t[:, j * pq : (j + 1) * pq], tt], axis=1).astype(BF)
 
     r3 = []
     for k in range(1, nq):
         to = (q + k) % nq
-        r3.append(reduce(sc.at[:, rows(to * qp, qp)], rq.at[k - 1], dev(zl=b * nq + to)))
+        r3.append(reduce(sc.at[:, to], rq.at[k - 1], dev(zl=b * nq + to)))
     for s in r3:
         s.wait_recv()
-    t = sc[:, rows(q * qp, qp)].astype(F32)
+    t = sc[:, q].astype(F32)
     for j in range(nq - 1):
         t += rq[j].astype(F32)
     se[...] = t.astype(BF)
@@ -342,19 +386,19 @@
     t = se[zh].astype(F32)
     for j in range(NZH * nb - 1):
         t += rb[j].astype(F32)
-    mine = rows(q * qp, qp)
-    ox[x, mine] = t.astype(BF)
-
-    ref = ox.at[x, mine]
-    step = [reduce(ref, ref, dev(zl=b * nq + (q + k) % nq)) for k in range(1, nq)]
+    t_proj = t[pq:qp]
+    ox[x, q] = t[0:pq].astype(BF)
+
+    step = [reduce(ox.at[x, q], ox.at[x, q], dev(zl=b * nq + (q + k) % nq)) for k in range(1, nq)]
+    last = [reduce(ox.at[x, q], ox.at[x, q], to) for to in near_x.values()]
+    for k, copy in enumerate(step, 1):
+        copy.wait_recv()
+        ref = ox.at[x, (q - k + nq) % nq]
+        last += [reduce(ref, ref, to) for to in near_x.values()]
     for s in a2:
         s.wait_recv()
     owned_ref[...] = av4[...]
-    for s in step:
-        s.wait_recv()
-    ref = ox.at[x, 0:xp]
-    step = [reduce(ref, ref, to) for to in near_x.values()]
-    for s in step:
+    for s in last:
         s.wait_recv()
 
     scale = 1.0 / (nx * nzl * NF)
@@ -362,7 +406,7 @@
     def unit(i):
         at = i * 16
         px, at = (at // xa, at % xa) if at < CUT else ((at - CUT) // xb, xa + (at - CUT) % xb)
-        return ox[px, at : at + 16, :].astype(F32) * scale
+        return ox[px, at // pq, at % pq : at % pq + 16, :].astype(F32) * scale
 
     for i in range(16):
         gdn_ref[16 * i : 16 * i + 16, 0:128] = unit(i)
@@ -370,7 +414,7 @@
         t = unit(32 + i)
         gup_ref[:, 256 * i : 256 * i + 128] = t[0:8]
         gup_ref[:, 256 * i + 128 : 256 * i + 256] = t[8:16]
-    gproj_ref[...] = unit(48)
+    gproj_ref[...] = t_proj * scale
     for s in pending:
         s.wait_send()
 
@@ -380,11 +424,11 @@
     nb = nzl // nq
     feats, width = embeddings.shape[1:]
     xa = CUT // nx
-    xb = 16 * -(-(ROWS - CUT) // (16 * nx))
-    qp = 16 * -(-(xa + xb) // (16 * nq))
-    padded = CUT + nx * xb
-    n_ag = 20 + (nq - 1) + (nx * NY - 1) + 3 + nx
-    n_rs = 2 + 2 * (NY - 1) + 3 * (nx - 1) + 2 * (nq - 1) + (NZH * nb - 1)
+    xb = (MAIN - CUT) // nx
+    pq = (xa + xb) // nq
+    qp = pq + ROWS - MAIN
+    n_ag = 21 + 2 * (nq - 1) + 2 * (nx * NY - 1) + 3 + 2 * nx
+    n_rs = 2 + 4 * (NY - 1) + 3 * (nx - 1) + 2 * (nq - 1) + (NZH * nb - 1) + nq * (nx - 1) + 3
     n_aa = nzl - 1 + nx - 1
     vmem = pl.BlockSpec(memory_space=pltpu.VMEM)
     return pl.pallas_call(
@@ -403,20 +447,23 @@
             pltpu.VMEM(owners.shape, jnp.int32),
             pltpu.VMEM(up_weight.shape, BF),
             pltpu.VMEM((NZH, NY, NC, ROWS, 128), BF),
-            pltpu.VMEM((NZH, NY, NC, padded, 128), BF),
-            pltpu.VMEM((NZH, NY, padded, 128), BF),
-            pltpu.VMEM((NY, NZH, padded, 128), BF),
+            pltpu.VMEM((NZH, NY, NC, ROWS, 128), BF),
+            pltpu.VMEM((NZH, NY, ROWS, 128), BF),
+            pltpu.VMEM((NY, NZH, ROWS, 128), BF),
             pltpu.VMEM((NY - 1, NZH, CUT, 128), BF),
             pltpu.VMEM((NZH, CUT, 128), BF),
             pltpu.VMEM((nx - 1, NZH, xa, 128), BF),
             pltpu.VMEM((nx - 1, NY, NZH, xb, 128), BF),
             pltpu.VMEM((NY, NZH, xb, 128), BF),
             pltpu.VMEM((NY - 1, NZH, xb, 128), BF),
-            pltpu.VMEM((NZH, nq * qp, 128), BF),
+            pltpu.VMEM((NY - 1, NZH, ROWS - MAIN, 128), BF),
+            pltpu.VMEM((NZH, ROWS - MAIN, 128), BF),
+            pltpu.VMEM((nx - 1, NZH, ROWS - MAIN, 128), BF),
+            pltpu.VMEM((NZH, nq, qp, 128), BF),
             pltpu.VMEM((nq - 1, NZH, qp, 128), BF),
             pltpu.VMEM((NZH, qp, 128), BF),
             pltpu.VMEM((NZH * nb - 1, qp, 128), BF),
-            pltpu.VMEM((nx, nq * qp, 128), BF),
+            pltpu.VMEM((nx, nq, pq, 128), BF),
             pltpu.VMEM((feats, 128), BF),
             pltpu.VMEM((128, feats), BF),
             pltpu.VMEM((feats, 128), F32),
@@ -435,7 +482,7 @@
             pltpu.SemaphoreType.DMA((n_aa,)),
         ],
         compiler_params=pltpu.CompilerParams(
-            collective_id=0, has_side_effects=True, vmem_limit_bytes=48 * 1024 * 1024
+            collective_id=0, has_side_effects=True, vmem_limit_bytes=56 * 1024 * 1024
         ),
         name="layer_backward",
     )(embeddings, cotangent, owners, projection, up_weight, down_weight)

time: 119 us -> 112 us (0.941)
  Pallas kernels: 110 us -> 106 us
  local copies, waits for them, and re-layouts: 7.52 us -> 3.59 us
    pallas_call x1, Pallas kernels: 110 us -> 106 us  [per_device(): pl.pallas_call(functools.partial(kernel, split), out_shape=(jax.ShapeDtyp...]
    unnamed x16 -> x10, local copies, waits for them, and re-layouts: 7.52 us -> 3.59 us
where the time goes in v3:
time: 112 us; the launch traced here: 110 us
  Pallas kernels  106 us (95%)
  local copies, waits for them, and re-layouts  3.59 us (3%)
    pallas_call x1, Pallas kernels, per_device(): pl.pallas_call(functools.partial(kernel, split), out_shape=(jax.ShapeDtyp...  106 us
    unnamed x10, local copies, waits for them, and re-layouts  3.59 us

profile of v3, /device:TPU:24, one launch (start us, length us, event | category | flops | bytes accessed | tf_op | source)
XLA Modules:
  0.0 110.4 jit_solution(8437539681332115153)
XLA Ops:
  0.6 106.2 %layer_backward.1 = (bf16[256,256]{1,0:T(8,128)(2,1)}, f32[16,128]{1,0:T(8,128)}, f32[8,4096]{1,0:T(8,128)}, f32[256,256]{1,0:T(8,128)}) custom-call(bf16[1,256,256]{2,1,0:T(8,128)(2,1)} %x_hbm.1, bf16[1,256,256]{2,1,0:T(8,128)(2,1)} %cot_hbm.1, s32[1,256]{1,0:T(1,128)} %own_hbm.1, bf16[16,128]{1,0:T(8,128)(2,1)} %proj_hbm.1, bf16[8,4096]{1,0:T(8,128)(2,1)} %up_hbm.1, ...), custom_call_target="tpu_custom_call" | custom-call | tf_op jit(solution)/shard_map/layer_backward/pallas_call | solution.py:434
  106.8 0.0 copy-start.2
  106.8 0.0 copy-start.1
  106.8 0.0 copy-start
  106.8 1.6 %copy.14 = bf16[256,256]{1,0:T(8,128)(2,1)} copy(bf16[256,256]{1,0:T(8,128)(2,1)} %get-tuple-element.8) | data formatting | bytes 262144
  108.5 0.0 copy-done.2
  108.5 0.6 copy.15
  109.1 0.0 copy-done.1
  109.1 0.7 copy.16
  109.7 0.0 copy-done
  109.7 0.7 copy.17
Async XLA Ops:
  106.8 1.7 %copy-start.2 = (f32[16,128]{1,0:T(8,128)S(1)}, f32[16,128]{1,0:T(8,128)}, u32[]{:S(2)}) copy-start(f32[16,128]{1,0:T(8,128)} %get-tuple-element.9) | copy-start | bytes 24580
  106.8 2.2 %copy-start.1 = (f32[8,4096]{1,0:T(8,128)S(1)}, f32[8,4096]{1,0:T(8,128)}, u32[]{:S(2)}) copy-start(f32[8,4096]{1,0:T(8,128)} %get-tuple-element.10) | copy-start | bytes 393220
  106.8 2.9 %copy-start = (f32[256,256]{1,0:T(8,128)S(1)}, f32[256,256]{1,0:T(8,128)}, u32[]{:S(2)}) copy-start(f32[256,256]{1,0:T(8,128)} %get-tuple-element.11) | copy-start | bytes 786436

commit v4 on v3

--- a/solution.py
+++ b/solution.py
@@ -25,7 +25,7 @@
     x_ref, cot_ref, own_ref, up_ref,
     wg, gg, rc, sa, rya, sba, rxa, rxb, sbb, ryb, ryt, st, rxt, sc, rq, se, rb, ox,
     nl, nlt, gn, av1, av2, av3, av4,
-    in_s, ag_s, ag_r, co_s, co_r, rs_s, rs_r, aa_s, aa_r,
+    in_s, ag_s, ag_r, co_s, co_r, rs_s, rs_r, aa_s, aa_r, met,
 ):
     nx, nzl, nq = split
     nb = nzl // nq
@@ -76,11 +76,21 @@
     peers += [
         dev(x=(x + i) % nx, y=(y + k) % NY) for i in range(nx) for k in range(NY) if i or k
     ]
-    peers += [dev(zl=(zl + k) % nzl) for k in range(1, nzl)]
-    peers += [dev(zh=1 - zh, zl=((b + k) % nb) * nq + q) for k in range(nb)]
-    half = ((zl + nzl // 2) % nzl)
+    peers += [dev(zl=b * nq + (q + k) % nq) for k in range(1, nq)]
+    m, nm = zh * nb + b, NZH * nb
+
+    def ring(k):
+        to = (m + k) % nm
+        return dev(zh=to // nb, zl=(to % nb) * nq + q)
+
+    peers += [ring(k) for k in range(1, nm) if min(k, nm - k) <= 2]
+    half = (zl + nzl // 2) % nzl
     if (nzl // 2) % nq:
         peers.append(dev(zh=1 - zh, zl=half))
+
+    def tell(i, to):
+        pl.semaphore_signal(met.at[i], inc=1, device_id=to, device_id_type=pl.DeviceIdType.MESH)
+
     for p in peers:
         pl.semaphore_signal(barrier, inc=1, device_id=p, device_id_type=pl.DeviceIdType.MESH)
 
@@ -108,8 +118,11 @@
     for copy in inputs[1:4]:
         copy.wait()
     pl.semaphore_wait(barrier, len(peers))
-
-    parts = ((CUT, (MAIN - CUT) // (nx * nq)), (0, CUT // (nx * nq)))
+    if nm > 5:
+        tell(0, ring(2))
+        tell(0, ring(nm - 2))
+
+    parts = ((CUT, (MAIN - CUT) // nx), (0, CUT // nx))
     main, tail = pl.ds(0, MAIN), pl.ds(MAIN, ROWS - MAIN)
     oz = 1 - zh
     own, other = wg.at[zh, y, c], wg.at[oz, y, c]
@@ -120,7 +133,7 @@
 
     far_main = []
     for base, size in parts:
-        far_main.append(swap(own.at[rows(base + (x * nq + half % nq) * size, size)], far))
+        far_main.append(swap(own.at[rows(base + x * size, size)], far))
         if base:
             far_tail = swap(own.at[tail], far)
     tails = [swap(own.at[tail], to) for to in near_y.values()]
@@ -130,28 +143,20 @@
     for k, copy in zip(near_y, tails):
         copy.wait_recv()
         to_core.append(swap(wg.at[zh, (y - k + NY) % NY, c, tail], sibling))
-    steps = []
+    shares = {}
     for n, (base, size) in enumerate(parts):
         far_main[n].wait_recv()
-        piece = rows(base + (x * nq + q) * size, size)
-        steps.append(
-            [swap(other.at[piece], dev(zl=b * nq + (q + k) % nq)) for k in range(1, nq)]
-        )
-        if n == 0:
-            far_tail.wait_recv()
-            tails = [swap(other.at[tail], to) for to in near_y.values()]
-            to_core.append(swap(other.at[tail], sibling))
-    shares = {}
-    for n, (base, size) in enumerate(parts):
-        for s in steps[n]:
-            s.wait_recv()
-        piece = rows(base + x * nq * size, nq * size)
+        piece = rows(base + x * size, size)
         for i in range(nx):
             for k in (1, 3, 2, 0):
                 if i or k:
                     shares[n, i, k] = swap(
                         other.at[piece], dev(x=(x + i) % nx, y=(y + k) % NY)
                     )
+        if n == 0:
+            far_tail.wait_recv()
+            tails = [swap(other.at[tail], to) for to in near_y.values()]
+            to_core.append(swap(other.at[tail], sibling))
     for k, copy in zip(near_y, tails):
         copy.wait_recv()
         to_core.append(swap(wg.at[oz, (y - k + NY) % NY, c, tail], sibling))
@@ -159,12 +164,17 @@
         copy.wait_recv()
         mains_core.append(swap(wg.at[zh, (y - k + NY) % NY, c, main], sibling))
 
+    if nm > 5:
+        pl.semaphore_wait(met.at[0], 2)
+        for k in range(1, nq):
+            tell(1, dev(zl=b * nq + (q + k) % nq))
+
     def to_sibling(n, i):
         base, size = parts[n]
         for k in range(NY):
             if i or k:
                 shares[n, i, k].wait_recv()
-        at = rows(base + ((x - i + nx) % nx) * nq * size, nq * size)
+        at = rows(base + ((x - i + nx) % nx) * size, size)
         return swap(wg.at[oz, :, c, at], sibling)
 
     for s in to_core:
@@ -187,28 +197,36 @@
     for s in mains_core:
         s.wait_recv()
 
-    def hidden_units(izh, iy, ic):
-        u = (izh * NY + iy) * NC + ic
-        urows = rows(512 + 16 * u, 16)
-        pieces = wg[:, :, :, urows, :].reshape(NF, 16, 128).astype(F32)
+    def hidden_units(izh, iy):
+        cores = (1 - c, c)
+        at = [rows(512 + 16 * ((izh * NY + iy) * NC + ic), 16) for ic in cores]
+        pieces = [wg[:, :, :, r, :].reshape(NF, 16, 128).astype(F32) for r in at]
         up = jnp.concatenate(
-            [pieces[:, 0:8].reshape(128, 128), pieces[:, 8:16].reshape(128, 128)], axis=1
+            [p[:, e : e + 8].reshape(128, 128) for p in pieces for e in (0, 8)], axis=1
         ).astype(BF)
-        down = jnp.concatenate([wg[izh, iy, ic, 0:256], wg[izh, iy, ic, 256:512]], axis=1)
+        downs = jnp.concatenate(
+            [
+                jnp.concatenate([wg[izh, iy, ic, 0:256], wg[izh, iy, ic, 256:512]], axis=1)
+                for ic in cores
+            ],
+            axis=0,
+        )
         cots = cot_ref[...]
         hidden = mm(nl[...], up)
         sig = 0.5 * jnp.tanh(0.5 * hidden) + 0.5
         act = (hidden * sig).astype(BF)
-        gh = (mm(cots, down, 1, 1) * sig * (1.0 + hidden * (1.0 - sig))).astype(BF)
+        gh = (mm(cots, downs, 1, 1) * sig * (1.0 + hidden * (1.0 - sig))).astype(BF)
+        gdn = mm(act, cots, 0, 0).astype(BF)
+        for e, ic in enumerate(cores):
+            gg[izh, iy, ic, 0:256] = gdn[256 * e : 256 * e + 256, 0:128]
+            gg[izh, iy, ic, 256:512] = gdn[256 * e : 256 * e + 256, 128:256]
         gn[...] += mm(gh, up, 1, 1)
         gup = mm(nlt[...], gh)
-        gup = jnp.concatenate(
-            [gup[:, 0:128].reshape(NF, 8, 128), gup[:, 128:256].reshape(NF, 8, 128)], axis=1
-        ).astype(BF)
-        gg[:, :, :, urows, :] = gup.reshape(NZH, NY, NC, 16, 128)
-        gdn = mm(act, cots, 0, 0).astype(BF)
-        gg[izh, iy, ic, 0:256] = gdn[:, 0:128]
-        gg[izh, iy, ic, 256:512] = gdn[:, 128:256]
+        for e, r in enumerate(at):
+            both = [gup[:, 256 * e + h : 256 * e + h + 128].reshape(NF, 8, 128) for h in (0, 128)]
+            gg[:, :, :, r, :] = (
+                jnp.concatenate(both, axis=1).astype(BF).reshape(NZH, NY, NC, 16, 128)
+            )
 
     down = pl.ds(0, CUT)
 
@@ -222,9 +240,8 @@
         @pl.loop(first, last)
         def _(i):
             izh = (zh + h) % NZH
-            hidden_units(izh, i, 1 - c)
+            hidden_units(izh, i)
             core_copy(h, i).start()
-            hidden_units(izh, i, c)
 
     r1a = []
 
@@ -293,6 +310,8 @@
     place = (owner - owner_x * nzl) * zrows + owner_x * per + within
     perm = jnp.where(row.astype(F32) == place, 1.0, 0.0).astype(BF)
     av1[...] = mm(perm, gemb).astype(BF)
+    if nm > 5:
+        pl.semaphore_wait(met.at[1], nq - 1)
     a1 = []
     mine = rows(zl * zrows, zrows)
     for k in range(1, nzl):
@@ -427,7 +446,7 @@
     xb = (MAIN - CUT) // nx
     pq = (xa + xb) // nq
     qp = pq + ROWS - MAIN
-    n_ag = 21 + 2 * (nq - 1) + 2 * (nx * NY - 1) + 3 + 2 * nx
+    n_ag = 21 + 2 * (nx * NY - 1) + 3 + 2 * nx
     n_rs = 2 + 4 * (NY - 1) + 3 * (nx - 1) + 2 * (nq - 1) + (NZH * nb - 1) + nq * (nx - 1) + 3
     n_aa = nzl - 1 + nx - 1
     vmem = pl.BlockSpec(memory_space=pltpu.VMEM)
@@ -480,6 +499,7 @@
             pltpu.SemaphoreType.DMA((n_rs,)),
             pltpu.SemaphoreType.DMA((n_aa,)),
             pltpu.SemaphoreType.DMA((n_aa,)),
+            pltpu.SemaphoreType.REGULAR((2,)),
         ],
         compiler_params=pltpu.CompilerParams(
             collective_id=0, has_side_effects=True, vmem_limit_bytes=56 * 1024 * 1024

time: 112 us -> 110 us (0.982)
  the two profiles are of different devices: /device:TPU:24 before, /device:TPU:4 now
where the time goes in v4:
time: 110 us
  Pallas kernels  106 us (96%)
  local copies, waits for them, and re-layouts  3.59 us (3%)
    pallas_call x1, Pallas kernels, per_device(): pl.pallas_call(functools.partial(kernel, split), out_shape=(jax.ShapeDtyp...  106 us
    unnamed x10, local copies, waits for them, and re-layouts  3.59 us

profile of v4, /device:TPU:4, one launch (start us, length us, event | category | flops | bytes accessed | tf_op | source)
XLA Modules:
  0.0 109.8 jit_solution(13486776249620063448)
XLA Ops:
  0.6 105.5 %layer_backward.1 = (bf16[256,256]{1,0:T(8,128)(2,1)}, f32[16,128]{1,0:T(8,128)}, f32[8,4096]{1,0:T(8,128)}, f32[256,256]{1,0:T(8,128)}) custom-call(bf16[1,256,256]{2,1,0:T(8,128)(2,1)} %x_hbm.1, bf16[1,256,256]{2,1,0:T(8,128)(2,1)} %cot_hbm.1, s32[1,256]{1,0:T(1,128)} %own_hbm.1, bf16[16,128]{1,0:T(8,128)(2,1)} %proj_hbm.1, bf16[8,4096]{1,0:T(8,128)(2,1)} %up_hbm.1, ...), custom_call_target="tpu_custom_call" | custom-call | tf_op jit(solution)/shard_map/layer_backward/pallas_call | solution.py:453
  106.1 0.0 copy-start.2
  106.2 0.0 copy-start.1
  106.2 0.0 copy-start
  106.2 1.6 %copy.14 = bf16[256,256]{1,0:T(8,128)(2,1)} copy(bf16[256,256]{1,0:T(8,128)(2,1)} %get-tuple-element.8) | data formatting | bytes 262144
  107.8 0.0 copy-done.2
  107.8 0.6 copy.15
  108.4 0.0 copy-done.1
  108.4 0.7 copy.16
  109.1 0.0 copy-done
  109.1 0.7 copy.17
Async XLA Ops:
  106.1 1.7 %copy-start.2 = (f32[16,128]{1,0:T(8,128)S(1)}, f32[16,128]{1,0:T(8,128)}, u32[]{:S(2)}) copy-start(f32[16,128]{1,0:T(8,128)} %get-tuple-element.9) | copy-start | bytes 24580
  106.2 2.2 %copy-start.1 = (f32[8,4096]{1,0:T(8,128)S(1)}, f32[8,4096]{1,0:T(8,128)}, u32[]{:S(2)}) copy-start(f32[8,4096]{1,0:T(8,128)} %get-tuple-element.10) | copy-start | bytes 393220
  106.2 2.9 %copy-start = (f32[256,256]{1,0:T(8,128)S(1)}, f32[256,256]{1,0:T(8,128)}, u32[]{:S(2)}) copy-start(f32[256,256]{1,0:T(8,128)} %get-tuple-element.11) | copy-start | bytes 786436

commit v5 on v4

--- a/solution.py
+++ b/solution.py
@@ -12,7 +12,9 @@
 SPLITS = {64: (4, 16, 4), 4: (2, 2, 2), 8: (2, 4, 2)}
 NZH, NY, NC = 2, 4, 2
 NF = NZH * NY * NC
-MAIN, ROWS, CUT = 768, 784, 512
+MAIN, ROWS = 768, 784
+CUT, DOWN = 384, 512
+HALF = (MAIN - DOWN) // 2
 
 
 def mm(a, b, ca=1, cb=0):
@@ -122,7 +124,7 @@
         tell(0, ring(2))
         tell(0, ring(nm - 2))
 
-    parts = ((CUT, (MAIN - CUT) // nx), (0, CUT // nx))
+    parts = ((DOWN, (MAIN - DOWN) // nx), (0, DOWN // nx))
     main, tail = pl.ds(0, MAIN), pl.ds(MAIN, ROWS - MAIN)
     oz = 1 - zh
     own, other = wg.at[zh, y, c], wg.at[oz, y, c]
@@ -228,7 +230,8 @@
                 jnp.concatenate(both, axis=1).astype(BF).reshape(NZH, NY, NC, 16, 128)
             )
 
-    down = pl.ds(0, CUT)
+    down, first = pl.ds(0, DOWN), pl.ds(0, CUT)
+    xd, xu = (DOWN - CUT) // nx, HALF // nx
 
     def core_copy(h, i):
         izh = (zh + h) % NZH
@@ -236,16 +239,24 @@
             gg.at[izh, i, 1 - c, down], rc.at[izh, i, down], co_s, co_r, h * NY + i, sibling
         )
 
-    def hidden_loop(h, first, last):
-        @pl.loop(first, last)
+    def hidden_loop(h):
+        @pl.loop(0, NY)
         def _(i):
             izh = (zh + h) % NZH
             hidden_units(izh, i)
             core_copy(h, i).start()
 
-    r1a = []
-
-    def down_sums(h):
+    def add(at):
+        sa_at, gg_at, rc_at = at
+        sa[sa_at] = (gg[gg_at].astype(F32) + rc[rc_at].astype(F32)).astype(BF)
+
+    r1a, r1b = [], []
+
+    def upper(h):
+        at = rows(DOWN + HALF * ((zh + h) % NZH), HALF)
+        return reduce(gg.at[:, :, 1 - c, at], rc.at[:, :, at], sibling)
+
+    def first_sums(h, r0):
         izh = (zh + h) % NZH
         for i in range(NY):
             core_copy(h, i).wait()
@@ -255,35 +266,36 @@
             @pl.loop(0, CUT // 128)
             def _(i, to=to):
                 r = rows(i * 128, 128)
-                sa[to, izh, r] = (
-                    gg[izh, to, c, r].astype(F32) + rc[izh, to, r].astype(F32)
-                ).astype(BF)
+                add(((to, izh, r), (izh, to, c, r), (izh, to, r)))
 
             if k:
-                r1a.append(reduce(sa.at[to, izh, down], rya.at[k - 1, izh], near_y[k]))
-
-    hidden_loop(0, 0, 2)
-    late = [to_sibling(1, i) for i in range(nx // 2)]
-    hidden_loop(0, 2, NY)
-    late += [to_sibling(1, i) for i in range(nx // 2, nx)]
-    down_sums(0)
+                r1a.append(reduce(sa.at[to, izh, first], rya.at[k - 1, izh], near_y[k]))
+        r0.wait_recv()
+        for k in [*range(1, nx), 0]:
+            to = (x + k) % nx
+            lo, hi = rows(CUT + to * xd, xd), rows(DOWN + HALF * izh + to * xu, xu)
+
+            @pl.loop(0, NY)
+            def _(i, lo=lo, hi=hi):
+                add(((i, izh, lo), (izh, i, c, lo), (izh, i, lo)))
+                for z in range(NZH):
+                    add(((i, z, hi), (z, i, c, hi), (z, i, hi)))
+
+            if k:
+                land = rxb.at[k - 1, :, izh, 0:xd]
+                r1b.append(reduce(sa.at[:, izh, lo], land, near_x[k]))
+                land = rxb.at[k - 1, :, :, rows(xd + xu * izh, xu)]
+                r1b.append(reduce(sa.at[:, :, hi], land, near_x[k]))
+
+    hidden_loop(0)
+    r0 = upper(0)
+    first_sums(0, r0)
+    late = [to_sibling(1, i) for i in range(nx)]
     for s in late:
         s.wait_recv()
-    hidden_loop(1, 0, NY)
-    upper = pl.ds(CUT, MAIN - CUT)
-    r0 = reduce(gg.at[:, :, 1 - c, upper], rc.at[:, :, upper], sibling)
-    down_sums(1)
-    r0.wait_recv()
-    r1b = []
-    for k in [*range(1, nx), 0]:
-        at = rows(CUT + ((x + k) % nx) * xb, xb)
-
-        @pl.loop(0, NY)
-        def _(i, at=at):
-            sa[i, :, at] = (gg[:, i, c, at].astype(F32) + rc[:, i, at].astype(F32)).astype(BF)
-
-        if k:
-            r1b.append(reduce(sa.at[:, :, at], rxb.at[k - 1], near_x[k]))
+    hidden_loop(1)
+    r0 = upper(1)
+    first_sums(1, r0)
 
     gnorm = gn[...]
     gfm = inv * (
@@ -340,10 +352,10 @@
             r2.append(reduce(sba.at[:, at], rxa.at[k - 1], near_x[k]))
     for s in r1b:
         s.wait_recv()
-    at = rows(CUT + x * xb, xb)
+    mine = (rows(CUT + x * xd, xd), rows(DOWN + x * xu, xu), rows(DOWN + HALF + x * xu, xu))
     for k in (1, 3, 2, 0):
         to = (y + k) % NY
-        t = sa[to, :, at].astype(F32)
+        t = jnp.concatenate([sa[to, :, at] for at in mine], axis=1).astype(F32)
         for j in range(nx - 1):
             t += rxb[j, to].astype(F32)
         sbb[to] = t.astype(BF)
@@ -424,7 +436,11 @@
 
     def unit(i):
         at = i * 16
-        px, at = (at // xa, at % xa) if at < CUT else ((at - CUT) // xb, xa + (at - CUT) % xb)
+        for base, size, off in (
+            (0, xa, 0), (CUT, xd, xa), (DOWN, xu, xa + xd), (DOWN + HALF, xu, xa + xd + xu)
+        ):
+            if base <= i * 16 < base + size * nx:
+                px, at = (i * 16 - base) // size, off + (i * 16 - base) % size
         return ox[px, at // pq, at % pq : at % pq + 16, :].astype(F32) * scale
 
     for i in range(16):
@@ -447,9 +463,13 @@
     pq = (xa + xb) // nq
     qp = pq + ROWS - MAIN
     n_ag = 21 + 2 * (nx * NY - 1) + 3 + 2 * nx
-    n_rs = 2 + 4 * (NY - 1) + 3 * (nx - 1) + 2 * (nq - 1) + (NZH * nb - 1) + nq * (nx - 1) + 3
+    n_rs = 3 + 4 * (NY - 1) + 6 * (nx - 1) + 2 * (nq - 1) + (NZH * nb - 1) + nq * (nx - 1) + 3
     n_aa = nzl - 1 + nx - 1
     vmem = pl.BlockSpec(memory_space=pltpu.VMEM)
+    operands = [
+        pltpu.with_memory_space_constraint(a, pltpu.HBM)
+        for a in (embeddings, cotangent, owners, projection, up_weight, down_weight)
+    ]
     return pl.pallas_call(
         functools.partial(kernel, split),
         out_shape=(
@@ -502,10 +522,10 @@
             pltpu.SemaphoreType.REGULAR((2,)),
         ],
         compiler_params=pltpu.CompilerParams(
-            collective_id=0, has_side_effects=True, vmem_limit_bytes=56 * 1024 * 1024
+            collective_id=0, has_side_effects=True, vmem_limit_bytes=48 * 1024 * 1024
         ),
         name="layer_backward",
-    )(embeddings, cotangent, owners, projection, up_weight, down_weight)
+    )(*operands)
 
 
 def solution(mesh):

time: 110 us -> 106 us (0.964)
  the two profiles are of different devices: /device:TPU:4 before, /device:TPU:20 now
where the time goes in v5:
time: 106 us
  Pallas kernels  103 us (97%)
  local copies, waits for them, and re-layouts  2.61 us (2%)
    pallas_call x1, Pallas kernels, per_device(): pl.pallas_call(functools.partial(kernel, split), out_shape=(jax.ShapeDtyp...  103 us
    unnamed x4, local copies, waits for them, and re-layouts  2.61 us

profile of v5, /device:TPU:20, one launch (start us, length us, event | category | flops | bytes accessed | tf_op | source)
XLA Modules:
  0.0 106.3 jit_solution(11183348739585674622)
XLA Ops:
  0.6 103.1 %layer_backward.1 = (bf16[256,256]{1,0:T(8,128)(2,1)S(1)}, f32[16,128]{1,0:T(8,128)S(1)}, f32[8,4096]{1,0:T(8,128)S(1)}, f32[256,256]{1,0:T(8,128)S(1)}) custom-call(bf16[1,256,256]{2,1,0:T(8,128)(2,1)} %x_hbm.1, bf16[1,256,256]{2,1,0:T(8,128)(2,1)} %cot_hbm.1, s32[1,256]{1,0:T(1,128)} %own_hbm.1, bf16[16,128]{1,0:T(8,128)(2,1)} %proj_hbm.1, ...), custom_call_target="tpu_custom_call" | custom-call | tf_op jit(solution)/shard_map/layer_backward/pallas_call | solution.py:473
  103.7 0.7 copy.14
  104.4 0.6 copy.15
  105.0 0.7 copy.16
  105.6 0.7 copy.17

commit v6 on v5

--- a/solution.py
+++ b/solution.py
@@ -26,7 +26,7 @@
     owned_ref, gproj_ref, gup_ref, gdn_ref,
     x_ref, cot_ref, own_ref, up_ref,
     wg, gg, rc, sa, rya, sba, rxa, rxb, sbb, ryb, ryt, st, rxt, sc, rq, se, rb, ox,
-    nl, nlt, gn, av1, av2, av3, av4,
+    nl, nlt, gn, half_cot, to_z, to_x, av1, av2, av3, av4,
     in_s, ag_s, ag_r, co_s, co_r, rs_s, rs_r, aa_s, aa_r, met,
 ):
     nx, nzl, nq = split
@@ -189,11 +189,27 @@
     centre = fm - jnp.mean(fm, axis=-1, keepdims=True)
     inv = lax.rsqrt(jnp.mean(centre * centre, axis=-1, keepdims=True) + 1e-05)
     normed = centre * inv
-    nl[...] = normed.astype(BF)
-    nlt[...] = normed.T.astype(BF)
+    normed_t = normed.T
+    nl[...] = (0.5 * normed_t).astype(BF)
+    nlt[...] = normed_t.astype(BF)
     gn[...] = jnp.zeros_like(gn)
     inputs[5].wait()
     inputs[6].wait()
+    half_cot[...] = (0.5 * cot_ref[...].astype(F32)).T.astype(BF)
+
+    row = lax.broadcasted_iota(jnp.int32, (feats, feats), 0)
+    col = lax.broadcasted_iota(jnp.int32, (feats, feats), 1)
+    across_f = jnp.broadcast_to(own_ref[...].astype(F32), (feats, feats))
+    down_f = jnp.sum(jnp.where(row == col, across_f, 0.0), axis=1, keepdims=True)
+    within = jnp.sum(
+        jnp.where((across_f == down_f) & (row < col), 1.0, 0.0), axis=0, keepdims=True
+    )
+    owner = across_f[0:1]
+    owner_x = jnp.floor(owner * (1.0 / nzl))
+    place = (owner - owner_x * nzl) * zrows + owner_x * per + within
+    to_z[...] = jnp.where(row.astype(F32) == place, 1.0, 0.0).astype(BF)
+    r_z, r_x, r_k = col // zrows, (col % zrows) // per, col % per
+    to_x[...] = jnp.where(row == r_x * (nzl * per) + r_z * per + r_k, 1.0, 0.0).astype(BF)
 
     mains_core += [to_sibling(0, i) for i in range(nx)]
     for s in mains_core:
@@ -214,16 +230,16 @@
             axis=0,
         )
         cots = cot_ref[...]
-        hidden = mm(nl[...], up)
-        sig = 0.5 * jnp.tanh(0.5 * hidden) + 0.5
-        act = (hidden * sig).astype(BF)
-        gh = (mm(cots, downs, 1, 1) * sig * (1.0 + hidden * (1.0 - sig))).astype(BF)
-        gdn = mm(act, cots, 0, 0).astype(BF)
+        half_hidden = mm(up, nl[...], 0, 0)
+        t1 = jnp.tanh(half_hidden) + 1.0
+        act32 = half_hidden * t1
+        gh = (mm(downs, half_cot[...]) * (t1 + act32 * (2.0 - t1))).astype(BF)
+        gdn = mm(act32.astype(BF), cots).astype(BF)
         for e, ic in enumerate(cores):
             gg[izh, iy, ic, 0:256] = gdn[256 * e : 256 * e + 256, 0:128]
             gg[izh, iy, ic, 256:512] = gdn[256 * e : 256 * e + 256, 128:256]
-        gn[...] += mm(gh, up, 1, 1)
-        gup = mm(nlt[...], gh)
+        gn[...] += mm(up, gh)
+        gup = mm(nlt[...], gh, 1, 1)
         for e, r in enumerate(at):
             both = [gup[:, 256 * e + h : 256 * e + h + 128].reshape(NF, 8, 128) for h in (0, 128)]
             gg[:, :, :, r, :] = (
@@ -297,7 +313,7 @@
     r0 = upper(1)
     first_sums(1, r0)
 
-    gnorm = gn[...]
+    gnorm = gn[...].T
     gfm = inv * (
         gnorm
         - jnp.mean(gnorm, axis=-1, keepdims=True)
@@ -310,18 +326,7 @@
     r0 = reduce(gg.at[:, :, 1 - c, tail], rc.at[:, :, tail], sibling)
     gemb = (mm(gfm, compressed, 1, 1) + mm(proj, gcomp, 1, 1)).astype(BF)
 
-    row = lax.broadcasted_iota(jnp.int32, (feats, feats), 0)
-    col = lax.broadcasted_iota(jnp.int32, (feats, feats), 1)
-    across_f = jnp.broadcast_to(own_ref[...].astype(F32), (feats, feats))
-    down_f = jnp.sum(jnp.where(row == col, across_f, 0.0), axis=1, keepdims=True)
-    within = jnp.sum(
-        jnp.where((across_f == down_f) & (row < col), 1.0, 0.0), axis=0, keepdims=True
-    )
-    owner = across_f[0:1]
-    owner_x = jnp.floor(owner * (1.0 / nzl))
-    place = (owner - owner_x * nzl) * zrows + owner_x * per + within
-    perm = jnp.where(row.astype(F32) == place, 1.0, 0.0).astype(BF)
-    av1[...] = mm(perm, gemb).astype(BF)
+    av1[...] = mm(to_z[...], gemb).astype(BF)
     if nm > 5:
         pl.semaphore_wait(met.at[1], nq - 1)
     a1 = []
@@ -395,15 +400,13 @@
     se[...] = t.astype(BF)
 
     r4 = []
-    for k in range(NZH * nb - 1, 0, -1):
+    for k in sorted(range(1, nm), key=lambda k: (k // nb == 0, k % nb != 0)):
         h2, b2 = (zh + k // nb) % NZH, (b + k % nb) % nb
         r4.append(reduce(se.at[h2], rb.at[k - 1], dev(zh=h2, zl=b2 * nq + q)))
 
     for s in a1:
         s.wait_recv()
-    r_z, r_x, r_k = col // zrows, (col % zrows) // per, col % per
-    perm = jnp.where(row == r_x * (nzl * per) + r_z * per + r_k, 1.0, 0.0).astype(BF)
-    av3[...] = mm(perm, av2[...]).astype(BF)
+    av3[...] = mm(to_x[...], av2[...]).astype(BF)
     a2 = []
     xrows = nzl * per
     mine = rows(x * xrows, xrows)
@@ -503,9 +506,12 @@
             pltpu.VMEM((NZH, qp, 128), BF),
             pltpu.VMEM((NZH * nb - 1, qp, 128), BF),
             pltpu.VMEM((nx, nq, pq, 128), BF),
-            pltpu.VMEM((feats, 128), BF),
             pltpu.VMEM((128, feats), BF),
-            pltpu.VMEM((feats, 128), F32),
+            pltpu.VMEM((128, feats), BF),
+            pltpu.VMEM((128, feats), F32),
+            pltpu.VMEM((width, feats), BF),
+            pltpu.VMEM((feats, feats), BF),
+            pltpu.VMEM((feats, feats), BF),
             pltpu.VMEM((feats, width), BF),
             pltpu.VMEM((feats, width), BF),
             pltpu.VMEM((feats, width), BF),

time: 106 us -> 107 us (level)
  the two profiles are of different devices: /device:TPU:20 before, /device:TPU:24 now
where the time goes in v6:
time: 107 us; the launch traced here: 105 us
  Pallas kernels  102 us (95%)
  local copies, waits for them, and re-layouts  2.61 us (2%)
    pallas_call x1, Pallas kernels, per_device(): pl.pallas_call(functools.partial(kernel, split), out_shape=(jax.ShapeDtyp...  102 us
    unnamed x4, local copies, waits for them, and re-layouts  2.61 us

profile of v6, /device:TPU:24, one launch (start us, length us, event | category | flops | bytes accessed | tf_op | source)
XLA Modules:
  0.0 104.8 jit_solution(13291532262815010001)
XLA Ops:
  0.6 101.6 %layer_backward.1 = (bf16[256,256]{1,0:T(8,128)(2,1)S(1)}, f32[16,128]{1,0:T(8,128)S(1)}, f32[8,4096]{1,0:T(8,128)S(1)}, f32[256,256]{1,0:T(8,128)S(1)}) custom-call(bf16[1,256,256]{2,1,0:T(8,128)(2,1)} %x_hbm.1, bf16[1,256,256]{2,1,0:T(8,128)(2,1)} %cot_hbm.1, s32[1,256]{1,0:T(1,128)} %own_hbm.1, bf16[16,128]{1,0:T(8,128)(2,1)} %proj_hbm.1, ...), custom_call_target="tpu_custom_call" | custom-call | tf_op jit(solution)/shard_map/layer_backward/pallas_call | solution.py:476
  102.2 0.7 copy.14
  102.9 0.6 copy.15
  103.5 0.7 copy.16
  104.1 0.7 copy.17

commit v7 on v6

--- a/solution.py
+++ b/solution.py
@@ -324,18 +324,6 @@
     gproj = mm(emb, gcomp).astype(BF)
     gg[:, :, :, MAIN:ROWS, :] = gproj.reshape(NZH, NY, NC, 16, 128)
     r0 = reduce(gg.at[:, :, 1 - c, tail], rc.at[:, :, tail], sibling)
-    gemb = (mm(gfm, compressed, 1, 1) + mm(proj, gcomp, 1, 1)).astype(BF)
-
-    av1[...] = mm(to_z[...], gemb).astype(BF)
-    if nm > 5:
-        pl.semaphore_wait(met.at[1], nq - 1)
-    a1 = []
-    mine = rows(zl * zrows, zrows)
-    for k in range(1, nzl):
-        to = (zl + k) % nzl
-        a1.append(exchange(av1.at[rows(to * zrows, zrows)], av2.at[mine], dev(zl=to)))
-    av2[mine] = av1[mine]
-
     r0.wait_recv()
     r1t = []
     for k in (1, 3, 2, 0):
@@ -373,6 +361,18 @@
         t += ryt[j].astype(F32)
     st[...] = t.astype(BF)
     r2 += [reduce(st, rxt.at[k - 1], near_x[k]) for k in range(1, nx)]
+    gemb = (mm(gfm, compressed, 1, 1) + mm(proj, gcomp, 1, 1)).astype(BF)
+
+    av1[...] = mm(to_z[...], gemb).astype(BF)
+    if nm > 5:
+        pl.semaphore_wait(met.at[1], nq - 1)
+    a1 = []
+    mine = rows(zl * zrows, zrows)
+    for k in range(1, nzl):
+        to = (zl + k) % nzl
+        a1.append(exchange(av1.at[rows(to * zrows, zrows)], av2.at[mine], dev(zl=to)))
+    av2[mine] = av1[mine]
+
     for s in r2:
         s.wait_recv()
     ta = sba[:, rows(x * xa, xa)].astype(F32)

time: 107 us -> 111 us (1.037); the launches traced: 105 us -> 111 us
  Pallas kernels: 102 us -> 107 us
    pallas_call x1, Pallas kernels: 102 us -> 107 us  [per_device(): pl.pallas_call(functools.partial(kernel, split), out_shape=(jax.ShapeDtyp...]
where the time goes in v7:
time: 111 us
  Pallas kernels  107 us (96%)
  local copies, waits for them, and re-layouts  2.61 us (2%)
    pallas_call x1, Pallas kernels, per_device(): pl.pallas_call(functools.partial(kernel, split), out_shape=(jax.ShapeDtyp...  107 us
    unnamed x4, local copies, waits for them, and re-layouts  2.61 us

profile of v7, /device:TPU:24, one launch (start us, length us, event | category | flops | bytes accessed | tf_op | source)
XLA Modules:
  0.0 110.6 jit_solution(8854172296303616370)
XLA Ops:
  0.6 107.3 %layer_backward.1 = (bf16[256,256]{1,0:T(8,128)(2,1)S(1)}, f32[16,128]{1,0:T(8,128)S(1)}, f32[8,4096]{1,0:T(8,128)S(1)}, f32[256,256]{1,0:T(8,128)S(1)}) custom-call(bf16[1,256,256]{2,1,0:T(8,128)(2,1)} %x_hbm.1, bf16[1,256,256]{2,1,0:T(8,128)(2,1)} %cot_hbm.1, s32[1,256]{1,0:T(1,128)} %own_hbm.1, bf16[16,128]{1,0:T(8,128)(2,1)} %proj_hbm.1, ...), custom_call_target="tpu_custom_call" | custom-call | tf_op jit(solution)/shard_map/layer_backward/pallas_call | solution.py:476
  108.0 0.7 copy.14
  108.6 0.6 copy.15
  109.2 0.7 copy.16
  109.9 0.7 copy.17
